TPU v7x, 128 devices: a whole 4x4x4 slice. The times are simulated.
128 devices in a mesh: seq: 16 (over y, z), req: 8 (over x, core).
Axes of the slice: x: 4, y: 4, z: 4, core: 2. Of those that a mesh axis runs over, the one named last changes fastest.
Arguments:
- span_queries: bfloat16 [1024, 8192], P('seq', 'req'), may hold values from -540 to 540
- span_key_value: bfloat16 [2, 1024, 1024], P(None, 'seq', 'req'), may hold values from -6 to 6
- prompt_key_value: bfloat16 [2, 16384, 1024], P(None, 'seq', 'req'), may hold values from -6 to 6
- span_start: int32 [1], replicated, may hold values from 15361 to 16384
- block_pool_key_value: bfloat16 [2048, 2, 64, 1024], P(('seq', 'req')), may hold values from -6 to 6
- block_dest: int32 [2048, 1], P(('seq', 'req')), may hold values from 0 to 15; in each aligned block of 16 rows (0 to 15, 16 to 31, ...) at most 4 rows name the same one
- block_request: int32 [2048], P(('seq', 'req')), may hold values from 0 to 1
- block_fill: int32 [2048], P(('seq', 'req')), may hold values from 1 to 64
- decode_query: bfloat16 [4, 256, 8192], P(None, ('seq', 'req')), may hold values from -540 to 540
- decoded_key_value: bfloat16 [4, 2, 256, 1024], P(None, None, ('seq', 'req')), may hold values from -6 to 6
Outputs:
- attended: bfloat16 [1024, 8192], P('seq', 'req')
- dec_out: bfloat16 [4, 256, 8192], P(None, ('seq', 'req'))
Inputs may be any that keep to these rules, and one draw needn't show every extreme that they name: `block_dest`: among the rows of one device no seq index is named more than 4 times, and one is named exactly 4 times.
All inputs are finite; a program needn't handle non-finite values.
Results may differ from a plain program's by a relative error of at most 0.0044.
Values may be sent and summed in bfloat16 or wider, within the bound.
A program may use at most 320 MiB of HBM per device.

v0:
```python
import jax
import jax.numpy as jnp
from jax import lax
from jax.sharding import PartitionSpec as P

QUERY_HEADS = 64
KEY_HEADS = 8
HEAD_WIDTH = 128
CAP = 4


MASK_NEGATIVE = -1e30


def merged_2(shard, axis, combine):
    everything = jax.tree.map(lambda part: lax.all_gather(part, axis), shard)
    initial = jax.tree.map(lambda part: part[0], everything)

    def lap(k, so_far):
        return combine(so_far, jax.tree.map(lambda part: part[k], everything))

    return lax.fori_loop(1, lax.axis_size(axis), lap, initial)


def fold_pair(first, second):
    max_one, sum_one, acc_one = first
    max_two, sum_two, acc_two = second
    joined = jnp.maximum(max_one, max_two)
    scale_one = jnp.exp(max_one - joined)
    scale_two = jnp.exp(max_two - joined)
    return (
        joined,
        sum_one * scale_one + sum_two * scale_two,
        acc_one * scale_one[..., None] + acc_two * scale_two[..., None],
    )


def soft_partial(scores, valid):
    masked = jnp.where(valid, scores, MASK_NEGATIVE)
    block_max = jnp.max(masked, axis=-1)
    probs = jnp.where(valid, jnp.exp(masked - block_max[..., None]), 0.0)
    block_sum = jnp.sum(probs, axis=-1)
    return (block_max, block_sum, probs.astype(jnp.bfloat16))


def block_partials(block_list, owners, fills, query_rows, owner_count):
    scale = HEAD_WIDTH ** (-0.5)
    picks = owners[:, None] == jnp.arange(owner_count, dtype=jnp.int32)[None, :]
    chosen = jnp.einsum(
        "br,trhgd->bthgd",
        picks.astype(jnp.bfloat16),
        query_rows,
        preferred_element_type=jnp.float32,
    ).astype(jnp.bfloat16)
    token_count = block_list.shape[0]
    token_slots = block_list.shape[2]
    key_rows = block_list[:, 0].reshape(token_count, token_slots, KEY_HEADS, HEAD_WIDTH)
    value_rows = block_list[:, 1].reshape(token_count, token_slots, KEY_HEADS, HEAD_WIDTH)
    scores = (
        jnp.einsum("bthgd,bkhd->bthgk", chosen, key_rows, preferred_element_type=jnp.float32)
        * scale
    )
    valid = (jnp.arange(token_slots, dtype=jnp.int32)[None, :] < fills[:, None])[
        :, None, None, None, :
    ]
    block_max, block_sum, weights = soft_partial(scores, valid)
    block_acc = jnp.einsum(
        "bthgk,bkhd->bthgd", weights, value_rows, preferred_element_type=jnp.float32
    )
    owned = picks[:, :, None, None, None]
    owner_max = jnp.max(jnp.where(owned, block_max[:, None], MASK_NEGATIVE), axis=0)
    each_max = jnp.max(jnp.where(owned, owner_max[None], MASK_NEGATIVE), axis=1)
    factor = jnp.exp(block_max - each_max)
    owned_float = picks.astype(jnp.float32)
    owner_sum = jnp.einsum(
        "br,bthg->rthg", owned_float, block_sum * factor, precision=lax.Precision.HIGHEST
    )
    owner_acc = jnp.einsum(
        "br,bthgd->rthgd",
        owned_float,
        block_acc * factor[..., None],
        precision=lax.Precision.HIGHEST,
    )
    return (owner_max, owner_sum, owner_acc)


def prefill(span_queries, span_key_value, prompt_key_value, span_start):
    head_group = QUERY_HEADS // KEY_HEADS
    scale = HEAD_WIDTH ** (-0.5)
    local_rows = span_queries.shape[0]
    kv_heads = span_key_value.shape[2] // HEAD_WIDTH
    all_query, all_kv = (
        lax.all_gather(span_queries, "seq", axis=0, tiled=True),
        lax.all_gather(span_key_value, "seq", axis=1, tiled=True),
    )
    span_len = all_query.shape[0]
    query_rows = all_query.reshape(span_len, kv_heads, head_group, HEAD_WIDTH)
    ctx_len = prompt_key_value.shape[1]
    width = min(512, ctx_len)
    token_count = ctx_len // width
    cache_keys = prompt_key_value[0].reshape(token_count, width, kv_heads, HEAD_WIDTH)
    cache_values = prompt_key_value[1].reshape(token_count, width, kv_heads, HEAD_WIDTH)
    offset = lax.axis_index("seq") * ctx_len
    start_pos = span_start[0]

    def cache_block(carry, item):
        block_idx, key_rows, value_rows = item
        scores = (
            jnp.einsum("qhgd,khd->qhgk", query_rows, key_rows, preferred_element_type=jnp.float32)
            * scale
        )
        positions = offset + block_idx * width + jnp.arange(width, dtype=jnp.int32)
        valid = (positions < start_pos)[None, None, None, :]
        block_max, block_sum, weights = soft_partial(scores, valid)
        block_acc = jnp.einsum(
            "qhgk,khd->qhgd", weights, value_rows, preferred_element_type=jnp.float32
        )
        return (fold_pair(carry, (block_max, block_sum, block_acc)), None)

    initial_state = (
        jnp.full((span_len, kv_heads, head_group), MASK_NEGATIVE, jnp.float32),
        jnp.zeros((span_len, kv_heads, head_group), jnp.float32),
        jnp.zeros((span_len, kv_heads, head_group, HEAD_WIDTH), jnp.float32),
    )
    part_all, _ = lax.scan(
        cache_block,
        initial_state,
        (jnp.arange(token_count, dtype=jnp.int32), cache_keys, cache_values),
    )
    part_max, part_sum, part_acc = part_all
    row_start = lax.axis_index("seq") * local_rows
    merged = merged_2((part_max, part_sum, part_acc), "seq", fold_pair)
    mine = tuple((lax.dynamic_slice_in_dim(piece, row_start, local_rows, 0) for piece in merged))
    own_query = span_queries.reshape(local_rows, kv_heads, head_group, HEAD_WIDTH)
    local_keys = all_kv[0].reshape(span_len, kv_heads, HEAD_WIDTH)
    local_values = all_kv[1].reshape(span_len, kv_heads, HEAD_WIDTH)
    scores = (
        jnp.einsum("qhgd,khd->qhgk", own_query, local_keys, preferred_element_type=jnp.float32)
        * scale
    )
    row_pos = row_start + jnp.arange(local_rows, dtype=jnp.int32)
    valid = (jnp.arange(span_len, dtype=jnp.int32)[None, :] <= row_pos[:, None])[:, None, None, :]
    own_max, own_sum, weights = soft_partial(scores, valid)
    own_acc = jnp.einsum(
        "qhgk,khd->qhgd", weights, local_values, preferred_element_type=jnp.float32
    )
    total = fold_pair(mine, (own_max, own_sum, own_acc))
    result = total[2] / total[1][..., None]
    return result.reshape(local_rows, kv_heads * head_group * HEAD_WIDTH).astype(jnp.bfloat16)


def decode(
    block_pool_key_value, block_dest, block_request, block_fill, decode_query, decoded_key_value
):
    head_group = QUERY_HEADS // KEY_HEADS
    scale = HEAD_WIDTH ** (-0.5)
    step_count = decode_query.shape[0]
    local_requests = decode_query.shape[1]
    query_rows = decode_query.reshape(step_count, local_requests, KEY_HEADS, head_group, HEAD_WIDTH)
    seq_count = lax.axis_size("seq")
    destination = block_dest[:, 0]
    pool_n = destination.shape[0]
    order = jnp.arange(pool_n, dtype=jnp.int32)
    same_dest = destination[:, None] == destination[None, :]
    earlier = order[None, :] < order[:, None]
    rank = jnp.sum((same_dest & earlier).astype(jnp.int32), axis=1)
    slot = destination * CAP + rank
    slot_ids = jnp.arange(seq_count * CAP, dtype=jnp.int32)
    match = slot_ids[:, None] == slot[None, :]
    source = jnp.sum(jnp.where(match, order[None, :], 0), axis=1)
    used = jnp.any(match, axis=1)
    send_blocks = block_pool_key_value[source]
    send_meta = jnp.stack([block_request[source], jnp.where(used, block_fill[source], 0)], axis=1)
    send_meta = send_meta.astype(jnp.float32).astype(jnp.bfloat16)
    got_blocks, got_meta = (
        lax.all_to_all(send_blocks, "seq", split_axis=0, concat_axis=0, tiled=True),
        lax.all_to_all(send_meta, "seq", split_axis=0, concat_axis=0, tiled=True),
    )
    got_meta = got_meta.astype(jnp.int32)
    cache_part = block_partials(
        got_blocks, got_meta[:, 0], got_meta[:, 1], query_rows, local_requests
    )
    fresh_keys = decoded_key_value[:, 0].reshape(step_count, local_requests, KEY_HEADS, HEAD_WIDTH)
    fresh_values = decoded_key_value[:, 1].reshape(
        step_count, local_requests, KEY_HEADS, HEAD_WIDTH
    )
    scores = (
        jnp.einsum("trhgd,urhd->rthgu", query_rows, fresh_keys, preferred_element_type=jnp.float32)
        * scale
    )
    order_steps = jnp.arange(step_count, dtype=jnp.int32)
    valid = (order_steps[None, :] <= order_steps[:, None])[None, :, None, None, :]
    new_max, new_sum, weights = soft_partial(scores, valid)
    new_acc = jnp.einsum(
        "rthgu,urhd->rthgd", weights, fresh_values, preferred_element_type=jnp.float32
    )
    total = fold_pair(cache_part, (new_max, new_sum, new_acc))
    result = total[2] / total[1][..., None]
    return (
        jnp.transpose(result, (1, 0, 2, 3, 4))
        .reshape(step_count, local_requests, QUERY_HEADS * HEAD_WIDTH)
        .astype(jnp.bfloat16)
    )


def on_device(
    span_queries,
    span_key_value,
    prompt_key_value,
    span_start,
    block_pool_key_value,
    block_dest,
    block_request,
    block_fill,
    decode_query,
    decoded_key_value,
):
    attended = prefill(span_queries, span_key_value, prompt_key_value, span_start)
    dec_out = decode(
        block_pool_key_value, block_dest, block_request, block_fill, decode_query, decoded_key_value
    )
    return (attended, dec_out)


def solution(mesh):
    placed = (
        P("seq", "req"),
        P(None, "seq", "req"),
        P(None, "seq", "req"),
        P(),
        P(("seq", "req"), None, None, None),
        P(("seq", "req"), None),
        P(("seq", "req")),
        P(("seq", "req")),
        P(None, ("seq", "req"), None),
        P(None, None, ("seq", "req"), None),
    )
    return jax.shard_map(
        on_device,
        mesh=mesh,
        in_specs=placed,
        out_specs=(P("seq", "req"), P(None, ("seq", "req"), None)),
        check_vma=False,
    )
```

profile of v0, /device:TPU:0, one launch (start us, length us, event | category | flops | bytes accessed | tf_op | source)
XLA Modules:
  0.0 965.5 jit_solution(17374847230909341077)
XLA Ops:
  8.0 1.1 fusion.126
  9.1 48.9 %all-gather.6.cloned.1.call-done = bf16[1024,1024]{1,0:T(8,128)(2,1)} async-done(((bf16[64,1024]{1,0:T(8,128)(2,1)}), bf16[1024,1024]{1,0:T(8,128)(2,1)}) %all-gather.6.cloned.1.call-update) | async-done | bytes 2097168 | tf_op jit(solution)/shard_map/all_gather | solution.py:93
  58.0 3.9 copy.170
  61.9 3.0 copy.171
  65.0 52.7 %while.35 = (s32[]{:T(128)}, f32[1024,1,8]{0,2,1:T(8,128)S(1)}, f32[1024,1,8]{0,2,1:T(8,128)S(1)}, f32[1024,1,8,128]{0,3,2,1:T(8,128)}, s32[2]{0:T(128)S(1)}, /*...) while((s32[]{:T(128)}, f32[1024,1,8]{0,2,1:T(8,128)S(1)}, ...), condition=%wide.region_3.4_spmd.clone, body=%wide.region_0.3_spmd.clone.sunk | while | flops 2206270464 | bytes 128813776 | solution.py:125
  67.0 2.5 bitcast_reduce_fusion.3
  69.5 5.7 copy-done.2
  75.2 4.6 fusion.145
  79.9 10.8 %bitcast_add_fusion.2 = f32[1024,1,8,128]{0,3,2,1:T(8,128)} fusion(f32[1024,1,8,128]{0,3,2,1:T(8,128)} %get-tuple-element.569, f32[512,1024,8]{1,0,2:T(8,128)} %copy-done.2, f32[1024,8]{0,1:T(8,128)S(1)} %get-tuple-element.547, pred[512]{0:T(512)(128)(4,1)S(1)} %add_compare_fusion.2, f32[1024,8]{0,1:T(8,128)S(1)} %get-tuple-element.551, ...), kind=kOutput, calls=%fused_computation.24.clone.1 | convolution fusion | flops 1098907648 | bytes 25396228 | tf_op jit(solution)/shard_map/while/body/eval_jaxpr/qhgk,khd->qhgd/dot_general | solution.py:115
  92.7 2.5 bitcast_reduce_fusion.3
  95.2 5.7 copy-done.2
  101.0 4.6 fusion.145
  105.7 12.0 %bitcast_add_fusion.2 = f32[1024,1,8,128]{0,3,2,1:T(8,128)} fusion(f32[1024,1,8,128]{0,3,2,1:T(8,128)} %get-tuple-element.569, f32[512,1024,8]{1,0,2:T(8,128)} %copy-done.2, f32[1024,8]{0,1:T(8,128)S(1)} %get-tuple-element.547, pred[512]{0:T(512)(128)(4,1)S(1)} %add_compare_fusion.2, f32[1024,8]{0,1:T(8,128)S(1)} %get-tuple-element.551, ...), kind=kOutput, calls=%fused_computation.24.clone.1 | convolution fusion | flops 1098907648 | bytes 25396228 | tf_op jit(solution)/shard_map/while/body/eval_jaxpr/qhgk,khd->qhgd/dot_general | solution.py:115
  120.7 4.9 all-to-all-start
  125.7 11.9 %gather_fusion.2 = bf16[64,2,64,1024]{3,2,1,0:T(8,128)(2,1)} fusion(bf16[16,2,64,1024]{3,2,1,0:T(8,128)(2,1)} %param.18, s32[1024]{0:T(1024)S(1)} %pad_clamp_fusion), kind=kCustom, calls=%fused_computation.2 | custom fusion | bytes 33554688 | tf_op jit(solution)/shard_map/gather | solution.py:172
  137.6 7.4 all-to-all-start.1
  145.3 379.4 %all_gather.31 = bf16[2,1024,128]{2,1,0:T(8,128)(2,1)S(1)} all-gather(bf16[2,64,128]{2,1,0:T(8,128)(2,1)S(1)} %copy-done.15), channel_id=1, replica_groups=mesh['seq'=16,'req'=8] {'seq'}, dimensions={1}, use_global_device_ids=true | all-gather | bytes 557056 | tf_op jit(solution)/shard_map/all_gather | solution.py:94
  526.3 1.0 fusion.93
  527.9 1.3 fusion.54
  529.6 3.3 convolution_convert_fusion
  532.9 24.6 %all-gather = f32[16384,1,8]{0,2,1:T(8,128)} all-gather(f32[1024,1,8]{0,2,1:T(8,128)S(1)} %get-tuple-element.234), channel_id=2, replica_groups=mesh['seq'=16,'req'=8] {'seq'}, dimensions={0}, use_global_device_ids=true | all-gather | bytes 557056 | tf_op jit(solution)/shard_map/all_gather | solution.py:16
  558.3 26.5 %all-gather.1 = f32[16384,1,8]{0,2,1:T(8,128)} all-gather(f32[1024,1,8]{0,2,1:T(8,128)S(1)} %get-tuple-element.235), channel_id=3, replica_groups=mesh['seq'=16,'req'=8] {'seq'}, dimensions={0}, use_global_device_ids=true | all-gather | bytes 557056 | tf_op jit(solution)/shard_map/all_gather | solution.py:16
  585.6 12.3 %fusion.125 = (bf16[64,1,64,1024]{3,2,1,0:T(8,128)(2,1)}, bf16[64,1,64,1024]{3,2,1,0:T(8,128)(2,1)}) fusion(bf16[64,2,64,1024]{3,2,1,0:T(8,128)(2,1)} %all-to-all-done.1), kind=kLoop, calls=%fused_computation.165 | loop fusion | bytes 33554432 | tf_op jit(solution)/shard_map/slice | solution.py:58
  597.9 9.1 copy.225
  607.0 7.7 bitcast_bitcast_fusion
  614.7 11.6 %bitcast_reduce_fusion.1 = (f32[64,4,8,8]{3,1,2,0:T(4,128)S(1)}, f32[64,8,64,4,8]{2,4,3,1,0:T(8,128)}) fusion(pred[64,64]{1,0:T(8,128)(4,1)S(1)} %iota_compare_fusion.1, bf16[64,4,8,8,128]{4,0,3,2,1:T(8,128)(2,1)} %convolution_convert_fusion, bf16[64,64,8,128,1]{3,2,1,0,4:T(8,128)(2,1)} %bitcast_bitcast_fusion), kind=kOutput, calls=%fused_computation.52 | convolution fusion | flops 271564800 | bytes 16846848 | tf_op jit(solution)/shard_map/bthgd,bkhd->bthgk/dot_general | solution.py:60
  626.9 17.8 %fusion.39 = f32[64,4,8,8]{3,1,2,0:T(4,128)} fusion(f32[64,8,64,4,8]{2,4,3,1,0:T(8,128)} %get-tuple-element.426, f32[64,4,8,8]{3,1,2,0:T(4,128)S(1)} %get-tuple-element.425, pred[64,64]{1,0:T(8,128)(4,1)S(1)} %iota_compare_fusion.1), kind=kLoop, calls=%fused_computation.62 | loop fusion | flops 5226496 | bytes 4329472 | tf_op jit(solution)/shard_map/reduce_sum | solution.py:42
  644.8 2.4 copy.201
  647.5 1.8 copy.191
  649.3 1.9 fusion.89
  651.1 1.4 fusion.100
  652.8 1.0 copy.200
  653.9 1.7 copy.204
  655.5 8.9 copy.224
  664.4 7.8 bitcast_bitcast_fusion.1
  672.1 8.5 bitcast_multiply_fusion.4
  680.7 7.1 fusion.82
  687.8 36.6 %all-gather.8.cloned.1.call-done = f32[16384,1,8,128]{0,3,2,1:T(8,128)} async-done(((f32[1024,1,8,128]{0,3,2,1:T(8,128)}), f32[16384,1,8,128]{0,3,2,1:T(8,128)}) %all-gather.8.cloned.1.call-update) | async-done | bytes 67108880 | tf_op jit(solution)/shard_map/all_gather | solution.py:16
  724.4 4.8 slice.63
  729.1 5.4 copy.173
  734.5 66.0 %copy.212 = f32[16384,1,8,128]{3,2,0,1:T(8,128)} copy(f32[16384,1,8,128]{0,3,2,1:T(8,128)} %all-gather.8.cloned.1.call-done) | data formatting | bytes 134217728 | tf_op jit(solution)/shard_map/while | solution.py:22
  800.5 153.4 %while.34 = (s32[]{:T(128)}, f32[1024,1,8]{0,2,1:T(8,128)S(1)}, f32[1024,1,8]{0,2,1:T(8,128)S(1)}, f32[1024,1,8,128]{3,2,1,0:T(8,128)}, f32[16,1024,1,8]{1,3,2,0...) while((s32[]{:T(128)}, f32[1024,1,8]{0,2,1:T(8,128)S(1)}, ...), condition=%wide.region_5.6_spmd, body=%wide.region_4.5_spmd.sunk | while | flops 3203077 | bytes 13205659 | solution.py:22
  801.2 0.8 fusion.140
  802.5 8.2 fusion.141
  811.5 0.8 fusion.140
  812.7 8.2 fusion.141
  821.7 0.8 fusion.140
  822.9 8.2 fusion.141
  831.9 0.8 fusion.140
  833.2 8.2 fusion.141
  842.2 0.8 fusion.140
  843.4 8.2 fusion.141
  852.4 0.8 fusion.140
  853.6 8.2 fusion.141
  863.8 8.2 fusion.141
  874.0 8.2 fusion.141
  884.3 8.2 fusion.141
  894.5 8.2 fusion.141
  904.7 8.2 fusion.141
  914.9 8.2 fusion.141
  925.2 8.2 fusion.141
  935.4 8.2 fusion.141
  945.6 8.2 fusion.141
  953.9 3.1 copy.177
  (170 shorter events, 38.5 us)
Async XLA Ops:
  7.2 110.8 %copy-start = (s32[16]{0:T(128)S(1)}, s32[16]{0:T(128)}, u32[]{:S(2)}) copy-start(s32[16]{0:T(128)} %param.21) | copy-start | bytes 196
  7.2 50.8 %all-gather.6.cloned.1.call-start = ((), (), s32[]{:S(2)}) async-start(), calls=%async_computation.2 | async-start | bytes 2228224 | tf_op jit(solution)/shard_map/all_gather | solution.py:93
  7.9 716.4 %all-gather.8.cloned.1.call-start = ((), (), s32[]{:S(2)}) async-start(), calls=%async_computation.3 | async-start | bytes 71303168 | tf_op jit(solution)/shard_map/all_gather | solution.py:16
  64.9 52.7 %copy-start.18 = (s32[16,1]{0,1:T(1,128)S(1)}, s32[16,1]{0,1:T(1,128)}, u32[]{:S(2)}) copy-start(s32[16,1]{0,1:T(1,128)} %param.19) | copy-start | bytes 196
  64.9 54.1 %copy-start.3 = (s32[16]{0:T(128)S(1)}, s32[16]{0:T(128)}, u32[]{:S(2)}) copy-start(s32[16]{0:T(128)} %param.20) | copy-start | bytes 196
  69.5 5.7 copy-start.2
  95.2 5.7 copy-start.2
  120.7 16.9 %all-to-all-start = ((bf16[16,4,2]{1,2,0:T(2,128)(2,1)}), bf16[16,4,2]{1,2,0:T(2,128)(2,1)S(1)}, u32[]{:S(2)}, u32[]{:S(2)}) async-start(bf16[16,4,2]{1,2,0:T(2,128)(2,1)} %copy.182), calls=%async_computation | async-start | bytes 16384 | tf_op jit(solution)/shard_map/all_to_all | solution.py:177
  137.6 7.4 copy-start.16
  137.6 7.5 copy-start.12
  137.6 7.7 copy-start.15
  137.6 389.8 %copy-start.11 = (bf16[64,1024]{1,0:T(8,128)(2,1)S(1)}, bf16[64,1024]{1,0:T(8,128)(2,1)}, u32[]{:S(2)}) copy-start(bf16[64,1024]{1,0:T(8,128)(2,1)} %param.14) | copy-start | bytes 393220
  137.6 447.9 %all-to-all-start.1 = ((bf16[64,2,64,1024]{3,2,1,0:T(8,128)(2,1)}), bf16[64,2,64,1024]{3,2,1,0:T(8,128)(2,1)}, u32[]{:S(2)}, u32[]{:S(2)}) async-start(bf16[64,2,64,1024]{3,2,1,0:T(8,128)(2,1)} %gather_fusion.2), calls=%async_computation.1 | async-start | bytes 33554432 | tf_op jit(solution)/shard_map/all_to_all | solution.py:176
  524.7 2.7 copy-start.4
  525.4 7.5 copy-start.13
  526.3 1.6 copy-start.8
  626.2 24.9 %copy-start.14 = (f32[2,4,8,8]{3,1,2,0:T(4,128)S(1)}, f32[2,4,8,8]{3,1,2,0:T(4,128)}, u32[]{:S(2)}) copy-start(f32[2,4,8,8]{3,1,2,0:T(4,128)} %copy-done.13) | copy-start | bytes 6148
  664.4 7.8 copy-start.7
  672.1 8.5 copy-start.6
  672.1 8.5 copy-start.10
  953.8 3.1 copy-start.17
  953.8 3.2 copy-start.5
  953.8 3.2 copy-start.9
  953.9 4.7 copy-start.1
Sparse Core Ops, SparseCore 0:
  10.2 47.7 all-gather.5
  117.8 606.5 all-gather.7
where the time goes:
time: 985 us; the launch traced here: 966 us
  blocking collectives  431 us (44%)
  other arithmetic  180 us (18%)
  local copies, waits for them, and re-layouts  177 us (18%)
  waiting for transfers between devices  86.2 us (9%)
  matrix products  63 us (6%)
  between operations  14.6 us (1%)
  starting transfers between devices  12.4 us (1%)
    all_gather x1, blocking collectives, prefill(): lax.all_gather(span_key_value, 'seq', axis=1, tiled=True)  379 us
    add x15, other arithmetic, fold_pair(): acc_one * scale_one[..., None] + acc_two * scale_two[..., None]  123 us
    while x3, local copies, waits for them, and re-layouts, merged_2(): return lax.fori_loop(1, lax.axis_size(axis), lap, initial)  74.4 us
    all_gather x2, blocking collectives, merged_2(): everything = jax.tree.map(lambda part: lax.all_gather(part, axis), shard)  51.1 us
    all_gather x1, waiting for transfers between devices, prefill(): lax.all_gather(span_queries, 'seq', axis=0, tiled=True)  48.9 us
    all_gather x1, waiting for transfers between devices, merged_2(): everything = jax.tree.map(lambda part: lax.all_gather(part, axis), shard)  36.6 us
    reduce_sum x5, other arithmetic, soft_partial(): block_sum = jnp.sum(probs, axis=-1)  29.2 us
    dot_general x2, matrix products, cache_block(): jnp.einsum('qhgk,khd->qhgd', weights, value_rows, preferred_element_type=...  22.7 us
  transfers between devices with their start and end apart: 4, of which 2 were waited for; matrix products, arithmetic and copies ran while one was open for 13% of the time, Pallas kernels for 0%

commit v1 on v0

v1 whole, which is shorter than its diff:
```python
import functools

import jax
import jax.numpy as jnp
from jax import lax
from jax.experimental import pallas as pl
from jax.experimental.pallas import tpu as pltpu
from jax.sharding import PartitionSpec as P

QUERY_HEADS = 64
KEY_HEADS = 8
HEAD_WIDTH = 128
HEAD_GROUP = QUERY_HEADS // KEY_HEADS
CAP = 4
SIDE = 4
HOMES = SIDE * SIDE

MASK_NEGATIVE = -1e30
EXP2_SCALE = HEAD_WIDTH ** (-0.5) * 1.4426950408889634
FAR_LAST = (1, 3, 2)
CHUNK = 256


def slots_kernel(dest_ref, request_ref, fill_ref, out_ref, count_ref):
    slots = HOMES * CAP

    def clear(i, _):
        out_ref[i] = 0
        out_ref[slots + i] = 0
        out_ref[2 * slots + i] = 0
        return 0

    lax.fori_loop(0, slots, clear, 0)
    for home in range(HOMES):
        count_ref[home] = 0

    def place(block, _):
        home = dest_ref[block]
        count = count_ref[home]
        slot = home * CAP + count
        out_ref[slot] = block
        out_ref[slots + slot] = request_ref[block]
        out_ref[2 * slots + slot] = fill_ref[block]
        count_ref[home] = count + 1
        return 0

    lax.fori_loop(0, dest_ref.shape[0], place, 0)


def block_slots(dest, request, fill):
    smem = pl.BlockSpec(memory_space=pltpu.SMEM)
    return pl.pallas_call(
        slots_kernel,
        out_shape=jax.ShapeDtypeStruct((3 * HOMES * CAP,), jnp.int32),
        in_specs=[smem] * 3,
        out_specs=smem,
        scratch_shapes=[pltpu.SMEM((HOMES,), jnp.int32)],
        name="block_slots",
    )(dest, request, fill)


def dot_nt(a, b):
    return lax.dot_general(a, b, (((1,), (1,)), ((), ())), preferred_element_type=jnp.float32)


def dot_nn(a, b):
    return lax.dot_general(a, b, (((1,), (0,)), ((), ())), preferred_element_type=jnp.float32)


def packed_stats(top, total):
    lane = lax.broadcasted_iota(jnp.int32, top.shape, 1)
    return jnp.where(lane < 4, top, total)


def merge(stats, parts):
    rows = stats[0].shape[1]
    tops = [jnp.broadcast_to(s[0:1], (8, rows)) for s in stats]
    sums = [jnp.broadcast_to(s[4:5], (8, rows)) for s in stats]
    top = functools.reduce(jnp.maximum, tops)
    weights = [jnp.exp2((t - top) * EXP2_SCALE) * s for t, s in zip(tops, sums)]
    total = functools.reduce(jnp.add, weights)
    inverse = 1.0 / jnp.where(total > 0.0, total, 1.0)
    out = None
    for weight, part in zip(weights, parts):
        share = jnp.broadcast_to((weight * inverse)[0:1], (128, rows))
        term = jnp.transpose(share) * part().astype(jnp.float32)
        out = term if out is None else out + term
    sub = lax.broadcasted_iota(jnp.int32, (8, rows), 0)
    return out, jnp.where(sub < 4, top, total)


def fused_kernel(
    sq_ref, skv_ref, pkv_ref, start_ref, pool_ref, slots_ref, dq_ref, dkv_ref,
    att_ref, dec_ref,
    qb, kv, kvs, vv, dqb, pool, acc, mx, col,
    pout, pst, pin, pinst,
    aout, aost, ain, ainst,
    bout, bost, bin_, binst,
    own_out,
    pool_sem, q_s, q_r, kv_s, kv_r, ks_s, ks_r, d_s, d_r, p_s, p_r, a_s, a_r, b_s, b_r,
):
    me = lax.axis_index("seq")
    y, z = me // SIDE, me % SIDE
    rows = sq_ref.shape[0]
    block = KEY_HEADS * rows
    keys = pkv_ref.shape[1]
    mesh_id = pl.DeviceIdType.MESH

    def at(dy, dz):
        return {"seq": (y + dy) % SIDE * SIDE + (z + dz) % SIDE}

    def remote(src, dst, send, recv, dy, dz):
        return pltpu.make_async_remote_copy(
            src_ref=src, dst_ref=dst, send_sem=send, recv_sem=recv,
            device_id=at(dy, dz), device_id_type=mesh_id,
        )

    pool_copy = pltpu.make_async_copy(pool_ref, pool, pool_sem)
    pool_copy.start()

    barrier = pltpu.get_barrier_semaphore()
    for o in (1, 2, 3):
        pl.semaphore_signal(barrier, inc=1, device_id=at(o, 0), device_id_type=mesh_id)
        pl.semaphore_signal(barrier, inc=1, device_id=at(0, o), device_id_type=mesh_id)

    for h in range(KEY_HEADS):
        qb[0, pl.ds(h * rows, rows), :] = sq_ref[:, pl.ds(h * HEAD_WIDTH, HEAD_WIDTH)]
    dqb[0, 0] = dq_ref[...]
    kvs[:, pl.ds(0, rows), :] = skv_ref[...]
    start = start_ref[0]
    position = me * keys + lax.broadcasted_iota(jnp.int32, (keys, HEAD_WIDTH), 0)
    own_keys = pkv_ref[0].astype(jnp.float32)
    kv[0, 0] = jnp.where(position < start, own_keys, own_keys[0:1]).astype(jnp.bfloat16)
    kv[0, 1] = jnp.where(position < start, pkv_ref[1].astype(jnp.float32), 0.0).astype(jnp.bfloat16)

    pl.semaphore_wait(barrier, 6)

    q_c, kv_c, ks_c, d_c, p_c, a_c, b_c = {}, {}, {}, {}, {}, {}, {}
    for o in FAR_LAST:
        q_c[o] = remote(qb.at[0], qb.at[o], q_s.at[o], q_r.at[o], o, 0)
        q_c[o].start()
        d_c[0, o] = remote(dqb.at[0, 0], dqb.at[0, o], d_s.at[0, o], d_r.at[0, o], 0, o)
        d_c[0, o].start()
    for o in FAR_LAST:
        d_c[o, 0] = remote(dqb.at[0, 0], dqb.at[o, 0], d_s.at[o, 0], d_r.at[o, 0], o, 0)
        d_c[o, 0].start()
        kv_c[o] = remote(kv.at[0], kv.at[o], kv_s.at[o], kv_r.at[o], 0, o)
        kv_c[o].start()
        ks_c[o] = remote(
            skv_ref, kvs.at[:, pl.ds(o * rows, rows), :], ks_s.at[o], ks_r.at[o], 0, o
        )
        ks_c[o].start()

    def load_values(oz):
        shard = y * SIDE + (z - oz + SIDE) % SIDE
        position = shard * keys + lax.broadcasted_iota(jnp.int32, (keys, HEAD_WIDTH), 0)
        vv[:, 0:HEAD_WIDTH] = kv[oz, 1]
        vv[:, HEAD_WIDTH:] = jnp.where(position < start, 1.0, 0.0).astype(jnp.bfloat16)

    def prompt_block(oz, oy_first, oy_count, first):
        def step(i, _):
            oy = oy_first + i // (block // CHUNK)
            here = pl.ds(pl.multiple_of(i % (block // CHUNK) * CHUNK, CHUNK), CHUNK)
            s = dot_nt(qb[oy, here, :], kv[oz, 0])
            top = jnp.broadcast_to(jnp.max(s, axis=1, keepdims=True), (CHUNK, HEAD_WIDTH))
            if not first:
                old = mx[oy, here, :]
                top = jnp.maximum(old, top)
            wide = jnp.concatenate([top] * (keys // HEAD_WIDTH), axis=1)
            p = jnp.exp2((s - wide) * EXP2_SCALE).astype(jnp.bfloat16)
            o = dot_nn(p, vv[...])
            if not first:
                keep = jnp.exp2((old - top) * EXP2_SCALE)
                o = o + acc[oy, here, :] * jnp.concatenate([keep, keep], axis=1)
            acc[oy, here, :] = o
            mx[oy, here, :] = top
            return 0

        lax.fori_loop(0, oy_count * (block // CHUNK), step, 0)

    def span_block(oy):
        width = SIDE * rows
        ones = jnp.ones((width, HEAD_WIDTH), jnp.bfloat16)
        values = jnp.concatenate([kvs[1], ones], axis=1)
        row_base = ((y - oy + SIDE) % SIDE * SIDE + z) * rows

        def step(i, _):
            here = pl.ds(pl.multiple_of(i * CHUNK, CHUNK), CHUNK)
            s = dot_nt(qb[oy, here, :], kvs[0])
            row = row_base + lax.broadcasted_iota(jnp.int32, (CHUNK, width), 0) % rows
            key = lax.broadcasted_iota(jnp.int32, (CHUNK, width), 1)
            key = (y * SIDE + (z - key // rows + SIDE) % SIDE) * rows + key % rows
            valid = key <= row
            s = jnp.where(valid, s, MASK_NEGATIVE)
            old = mx[oy, here, :]
            top = jnp.maximum(
                old, jnp.broadcast_to(jnp.max(s, axis=1, keepdims=True), (CHUNK, HEAD_WIDTH))
            )
            wide = jnp.concatenate([top] * (width // HEAD_WIDTH), axis=1)
            p = jnp.where(valid, jnp.exp2((s - wide) * EXP2_SCALE), 0.0).astype(jnp.bfloat16)
            o = dot_nn(p, values)
            keep = jnp.exp2((old - top) * EXP2_SCALE)
            o = o + acc[oy, here, :] * jnp.concatenate([keep, keep], axis=1)
            total = o[:, HEAD_WIDTH:]
            pout[oy, here, :] = (o[:, :HEAD_WIDTH] / total).astype(jnp.bfloat16)
            col[here, :] = packed_stats(top, total)
            return 0

        lax.fori_loop(0, block // CHUNK, step, 0)
        pst[oy] = jnp.transpose(col[...])[0:8]

    pair_rows = block // KEY_HEADS
    window = CAP * pool.shape[2]

    def decode_home(oy, oz):
        home = (y - oy + SIDE) % SIDE * SIDE + (z - oz + SIDE) % SIDE
        first = home * CAP
        index = [slots_ref[first + c] for c in range(CAP)]
        row = lax.broadcasted_iota(jnp.int32, (pair_rows, window), 0)
        key = lax.broadcasted_iota(jnp.int32, (pair_rows, window), 1)
        which = key // pool.shape[2]
        request = jnp.zeros((pair_rows, window), jnp.int32)
        fill = jnp.zeros((pair_rows, window), jnp.int32)
        for c in range(CAP):
            request = jnp.where(which == c, slots_ref[HOMES * CAP + first + c], request)
            fill = jnp.where(which == c, slots_ref[2 * HOMES * CAP + first + c], fill)
        valid = (row // (pair_rows // 2) == request) & (key % pool.shape[2] < fill)
        valid_float = jnp.where(valid, 1.0, 0.0)
        ones = jnp.ones((window, HEAD_WIDTH), jnp.bfloat16)

        def step(h, _):
            lanes = pl.ds(pl.multiple_of(h * HEAD_WIDTH, HEAD_WIDTH), HEAD_WIDTH)
            here = pl.ds(pl.multiple_of(h * pair_rows, pair_rows), pair_rows)
            k = jnp.concatenate([pool[i, 0, :, lanes] for i in index], axis=0)
            v = jnp.concatenate([pool[i, 1, :, lanes] for i in index], axis=0)
            ok = valid_float > 0.5
            s = jnp.where(ok, dot_nt(dqb[oy, oz, here, :], k), MASK_NEGATIVE)
            top = jnp.max(s, axis=1, keepdims=True)
            p = jnp.where(ok, jnp.exp2((s - top) * EXP2_SCALE), 0.0).astype(jnp.bfloat16)
            o = dot_nn(p, jnp.concatenate([v, ones], axis=1))
            total = o[:, HEAD_WIDTH:]
            out = o[:, :HEAD_WIDTH] / jnp.where(total > 0.0, total, 1.0)
            aout[oz, oy, here, :] = out.astype(jnp.bfloat16)
            col[here, :] = packed_stats(jnp.broadcast_to(top, total.shape), total)
            return 0

        lax.fori_loop(0, KEY_HEADS, step, 0, unroll=2)
        aost[oz, oy] = jnp.transpose(col[...])[0:8]

    def send_decode(oy, oz):
        for i, (out, into) in enumerate(((aout, ain), (aost, ainst))):
            c = remote(out.at[oz, oy], into.at[oz, oy], a_s.at[oz, oy, i], a_r.at[oz, oy, i],
                       0, SIDE - oz)
            c.start()
            a_c[oz, oy, i] = c

    load_values(0)
    prompt_block(0, 0, 1, True)
    for o in FAR_LAST:
        d_c[0, o].wait_recv()
        for oy in FAR_LAST:
            d_c[oy, o] = remote(
                dqb.at[0, o], dqb.at[oy, o], d_s.at[oy, o], d_r.at[oy, o], oy, 0
            )
            d_c[oy, o].start()
    for oy in FAR_LAST:
        q_c[oy].wait_recv()
        prompt_block(0, oy, 1, True)

    pool_copy.wait()
    decode_home(0, 0)
    for oz in FAR_LAST:
        decode_home(0, oz)
        send_decode(0, oz)
    for oy in FAR_LAST:
        d_c[oy, 0].wait_recv()
        decode_home(oy, 0)

    for oz in FAR_LAST:
        kv_c[oz].wait_recv()
        load_values(oz)
        prompt_block(oz, 0, SIDE, False)
        if oz != FAR_LAST[-1]:
            for oy in FAR_LAST:
                d_c[oy, oz].wait_recv()
                decode_home(oy, oz)
                send_decode(oy, oz)

    for oz in FAR_LAST:
        ks_c[oz].wait_recv()
    for oy in (2, 1, 3):
        span_block(oy)
        for i, (out, into) in enumerate(((pout, pin), (pst, pinst))):
            c = remote(out.at[oy], into.at[oy], p_s.at[oy, i], p_r.at[oy, i], SIDE - oy, 0)
            c.start()
            p_c[oy, i] = c
    for oy in FAR_LAST:
        d_c[oy, FAR_LAST[-1]].wait_recv()
        decode_home(oy, FAR_LAST[-1])
        send_decode(oy, FAR_LAST[-1])
    span_block(0)

    extra = dkv_ref.shape[2]
    row = lax.broadcasted_iota(jnp.int32, (pair_rows, extra), 0)
    key = lax.broadcasted_iota(jnp.int32, (pair_rows, extra), 1)
    step_of_row = row % (pair_rows // 2) // HEAD_GROUP
    fresh = (row // (pair_rows // 2) == key // (extra // 2)) & (key % (extra // 2) <= step_of_row)
    ones = jnp.ones((extra, HEAD_WIDTH), jnp.bfloat16)
    for h in range(KEY_HEADS):
        here = pl.ds(h * pair_rows, pair_rows)
        s = jnp.where(fresh, dot_nt(dqb[0, 0, here, :], dkv_ref[0, h]), MASK_NEGATIVE)
        top = jnp.max(s, axis=1, keepdims=True)
        p = jnp.where(fresh, jnp.exp2((s - top) * EXP2_SCALE), 0.0).astype(jnp.bfloat16)
        o = dot_nn(p, jnp.concatenate([dkv_ref[1, h], ones], axis=1))
        total = o[:, HEAD_WIDTH:]
        own_out[here, :] = o[:, :HEAD_WIDTH] / total
        col[here, :] = packed_stats(jnp.broadcast_to(top, total.shape), total)
    own_stats = jnp.transpose(col[...])[0:8]

    for oy in (2, 1, 3, 0):
        for oz in FAR_LAST:
            a_c[oz, oy, 0].wait_recv()
            a_c[oz, oy, 1].wait_recv()
        out, stats = merge(
            [aost[0, oy]] + [ainst[oz, oy] for oz in FAR_LAST],
            [lambda oy=oy: aout[0, oy]]
            + [lambda oz=oz, oy=oy: ain[oz, oy] for oz in FAR_LAST],
        )
        bout[oy] = out.astype(jnp.bfloat16)
        bost[oy] = stats
        if oy:
            for i, (out_ref, into) in enumerate(((bout, bin_), (bost, binst))):
                c = remote(out_ref.at[oy], into.at[oy], b_s.at[oy, i], b_r.at[oy, i], SIDE - oy, 0)
                c.start()
                b_c[oy, i] = c

    for oy in FAR_LAST:
        p_c[oy, 0].wait_recv()
        p_c[oy, 1].wait_recv()
    out, _ = merge(
        [pst[0]] + [pinst[oy] for oy in FAR_LAST],
        [lambda: pout[0]] + [lambda oy=oy: pin[oy] for oy in FAR_LAST],
    )
    out = out.astype(jnp.bfloat16)
    for h in range(KEY_HEADS):
        att_ref[:, pl.ds(h * HEAD_WIDTH, HEAD_WIDTH)] = out[h * rows : (h + 1) * rows]

    for oy in FAR_LAST:
        b_c[oy, 0].wait_recv()
        b_c[oy, 1].wait_recv()
    out, _ = merge(
        [own_stats, bost[0]] + [binst[oy] for oy in FAR_LAST],
        [lambda: own_out[...], lambda: bout[0]] + [lambda oy=oy: bin_[oy] for oy in FAR_LAST],
    )
    dec_ref[...] = out.astype(jnp.bfloat16)

    for copies in (q_c, kv_c, ks_c, d_c, p_c, a_c, b_c):
        for c in copies.values():
            c.wait_send()


def on_device(
    span_queries,
    span_key_value,
    prompt_key_value,
    span_start,
    block_pool_key_value,
    block_dest,
    block_request,
    block_fill,
    decode_query,
    decoded_key_value,
):
    steps, requests = decode_query.shape[:2]
    rows = span_queries.shape[0]
    block = KEY_HEADS * rows
    keys = prompt_key_value.shape[1]
    slots = block_slots(block_dest[:, 0], block_request, block_fill)
    dq = decode_query.reshape(steps, requests, KEY_HEADS, HEAD_GROUP, HEAD_WIDTH)
    dq = dq.transpose(2, 1, 0, 3, 4).reshape(block, HEAD_WIDTH)
    dkv = decoded_key_value.reshape(steps, 2, requests, KEY_HEADS, HEAD_WIDTH)
    dkv = dkv.transpose(1, 3, 2, 0, 4)
    dkv = jnp.pad(dkv, ((0, 0), (0, 0), (0, 0), (0, 8 - steps), (0, 0)))
    dkv = dkv.reshape(2, KEY_HEADS, 8 * requests, HEAD_WIDTH)

    bf, f32 = jnp.bfloat16, jnp.float32
    part = (block, HEAD_WIDTH)
    stat = (8, block)
    vmem = pl.BlockSpec(memory_space=pltpu.VMEM)
    smem = pl.BlockSpec(memory_space=pltpu.SMEM)
    dma = pltpu.SemaphoreType.DMA
    attended, dec = pl.pallas_call(
        fused_kernel,
        out_shape=(
            jax.ShapeDtypeStruct(span_queries.shape, bf),
            jax.ShapeDtypeStruct(part, bf),
        ),
        in_specs=[vmem, vmem, vmem, smem, pl.BlockSpec(memory_space=pl.ANY), smem, vmem, vmem],
        out_specs=(vmem, vmem),
        scratch_shapes=[
            pltpu.VMEM((SIDE,) + part, bf),
            pltpu.VMEM((SIDE, 2, keys, HEAD_WIDTH), bf),
            pltpu.VMEM((2, SIDE * rows, HEAD_WIDTH), bf),
            pltpu.VMEM((keys, 2 * HEAD_WIDTH), bf),
            pltpu.VMEM((SIDE, SIDE) + part, bf),
            pltpu.VMEM(block_pool_key_value.shape, bf),
            pltpu.VMEM((SIDE, block, 2 * HEAD_WIDTH), f32),
            pltpu.VMEM((SIDE,) + part, f32),
            pltpu.VMEM(part, f32),
            pltpu.VMEM((SIDE,) + part, bf),
            pltpu.VMEM((SIDE,) + stat, f32),
            pltpu.VMEM((SIDE,) + part, bf),
            pltpu.VMEM((SIDE,) + stat, f32),
            pltpu.VMEM((SIDE, SIDE) + part, bf),
            pltpu.VMEM((SIDE, SIDE) + stat, f32),
            pltpu.VMEM((SIDE, SIDE) + part, bf),
            pltpu.VMEM((SIDE, SIDE) + stat, f32),
            pltpu.VMEM((SIDE,) + part, bf),
            pltpu.VMEM((SIDE,) + stat, f32),
            pltpu.VMEM((SIDE,) + part, bf),
            pltpu.VMEM((SIDE,) + stat, f32),
            pltpu.VMEM(part, f32),
            dma,
            dma((SIDE,)), dma((SIDE,)),
            dma((SIDE,)), dma((SIDE,)),
            dma((SIDE,)), dma((SIDE,)),
            dma((SIDE, SIDE)), dma((SIDE, SIDE)),
            dma((SIDE, 2)), dma((SIDE, 2)),
            dma((SIDE, SIDE, 2)), dma((SIDE, SIDE, 2)),
            dma((SIDE, 2)), dma((SIDE, 2)),
        ],
        compiler_params=pltpu.CompilerParams(
            collective_id=0, has_side_effects=True, vmem_limit_bytes=48 * 1024 * 1024
        ),
        name="span_and_decode",
    )(span_queries, span_key_value, prompt_key_value, span_start, block_pool_key_value, slots,
      dq, dkv)
    dec = dec.reshape(KEY_HEADS, requests, steps, HEAD_GROUP, HEAD_WIDTH)
    dec = dec.transpose(2, 1, 0, 3, 4).reshape(steps, requests, QUERY_HEADS * HEAD_WIDTH)
    return attended, dec


def solution(mesh):
    placed = (
        P("seq", "req"),
        P(None, "seq", "req"),
        P(None, "seq", "req"),
        P(),
        P(("seq", "req"), None, None, None),
        P(("seq", "req"), None),
        P(("seq", "req")),
        P(("seq", "req")),
        P(None, ("seq", "req"), None),
        P(None, None, ("seq", "req"), None),
    )
    return jax.shard_map(
        on_device,
        mesh=mesh,
        in_specs=placed,
        out_specs=(P("seq", "req"), P(None, ("seq", "req"), None)),
        check_vma=False,
    )
```

time: 985 us -> 99.9 us (0.10); the launches traced: 966 us -> 99.5 us
  blocking collectives: 431 us -> 0 us
  other arithmetic: 180 us -> 0 us
  local copies, waits for them, and re-layouts: 177 us -> 8.8 us
  Pallas kernels: 0 us -> 89.3 us
  waiting for transfers between devices: 86.2 us -> 0 us
  matrix products: 63 us -> 0 us
  between operations: 14.6 us -> 1.34 us
  starting transfers between devices: 12.4 us -> 0 us
    all_gather x3 -> x0, blocking collectives: 431 us -> none  [the longest x1 379 us: prefill(): lax.all_gather(span_key_value, 'seq', axis=1, tiled=True)]
    add x18 -> x0, other arithmetic: 125 us -> none  [the longest x15 123 us: fold_pair(): acc_one * scale_one[..., None] + acc_two * scale_two[..., None]]
    pallas_call x0 -> x2, Pallas kernels: none -> 89.3 us  [the longest x1 87.4 us: on_device(): pl.pallas_call(fused_kernel, out_shape=(jax.ShapeDtypeStruct(span_queries...]
    while x24 -> x0, local copies, waits for them, and re-layouts: 85.9 us -> none  [the longest x3 74.4 us: merged_2(): return lax.fori_loop(1, lax.axis_size(axis), lap, initial)]
    all_gather x2 -> x0, waiting for transfers between devices: 85.5 us -> none  [the longest x1 48.9 us: prefill(): lax.all_gather(span_queries, 'seq', axis=0, tiled=True)]
    dot_general x13 -> x0, matrix products: 63 us -> none  [the longest x2 22.7 us: cache_block(): jnp.einsum('qhgk,khd->qhgd', weights, value_rows, preferred_element_type=...]
    reduce_sum x7 -> x0, other arithmetic: 29.4 us -> none  [the longest x5 29.2 us: soft_partial(): block_sum = jnp.sum(probs, axis=-1)]
    mul x35 -> x0, other arithmetic: 24 us -> none  [the longest x17 12.2 us: fold_pair(): acc_two * scale_two[..., None]]
  transfers between devices with their start and end apart: 4 -> 0, of which waited for: 2 -> 0; matrix products, arithmetic and copies ran while one was open for 13% -> 0% of each run, Pallas kernels for 0% -> 0%
where the time goes in v1:
time: 99.9 us; the launch traced here: 99.5 us
  Pallas kernels  89.3 us (89%)
  local copies, waits for them, and re-layouts  8.8 us (9%)
  between operations  1.34 us (1%)
    pallas_call x1, Pallas kernels, on_device(): pl.pallas_call(fused_kernel, out_shape=(jax.ShapeDtypeStruct(span_queries...  87.4 us
    unnamed x11, local copies, waits for them, and re-layouts  6.22 us

profile of v1, /device:TPU:0, one launch (start us, length us, event | category | flops | bytes accessed | tf_op | source)
XLA Modules:
  0.0 99.5 jit_solution(12482421477261761470)
XLA Ops:
  1.3 1.9 %block_slots.1.slots_ref = s32[192]{0:T(256)} custom-call(s32[16]{0:T(128)} %bitcast.17, s32[16]{0:T(128)} %request_ref.1, s32[16]{0:T(128)} %fill_ref.1), custom_call_target="tpu_custom_call" | custom-call | tf_op jit(solution)/shard_map/block_slots/pallas_call | solution.py:52
  3.2 0.8 reshape.24
  4.1 1.0 %reshape.22 = bf16[4,2,8,8,128]{4,3,2,1,0:T(8,128)(2,1)S(1)} reshape(bf16[4,2,8192]{2,1,0:T(2,128)(2,1)} %param.18) | data formatting | bytes 262144 | tf_op jit(solution)/shard_map/reshape | solution.py:379
  5.1 0.0 copy-start
  5.1 2.2 %copy-done = bf16[16,2,64,1024]{3,2,1,0:T(8,128)(2,1)S(1)} copy-done((bf16[16,2,64,1024]{3,2,1,0:T(8,128)(2,1)S(1)}, bf16[16,2,64,1024]{3,2,1,0:T(8,128)(2,1)}, u32[]{:S(2)}) %copy-start) | copy-done | bytes 4194328
  7.3 0.0 copy-start.1
  7.3 1.0 %copy-done.1 = bf16[2,1024,128]{2,1,0:T(8,128)(2,1)S(1)} copy-done((bf16[2,1024,128]{2,1,0:T(8,128)(2,1)S(1)}, bf16[2,1024,128]{2,1,0:T(8,128)(2,1)}, u32[]{:S(2)}) %copy-start.1) | copy-done | bytes 524312
  8.4 0.0 copy-start.2
  8.4 0.9 copy-done.2
  9.3 0.0 copy-start.3
  9.3 0.8 copy-done.3
  10.0 0.0 copy-start.4
  10.0 0.7 copy-done.4
  10.7 87.4 %span_and_decode.1 = (bf16[64,1024]{1,0:T(8,128)(2,1)S(1)}, bf16[512,128]{1,0:T(8,128)(2,1)S(1)}) custom-call(bf16[64,1024]{1,0:T(8,128)(2,1)S(1)} %copy-done.2, bf16[2,64,128]{2,1,0:T(8,128)(2,1)S(1)} %copy-done.3, bf16[2,1024,128]{2,1,0:T(8,128)(2,1)S(1)} %copy-done.1, s32[1]{0:T(128)S(6)} %copy.18.start_ref, bf16[16,2,64,1024]{3,2,1,0:T(8,128)(2,1)S(1)} %copy-done, ...), custom_call_target="tpu_custom_call" | custom-call | tf_op jit(solution)/shard_map/span_and_decode/pallas_call | solution.py:392
  98.1 0.7 reshape.27
  98.8 0.7 copy.19
  (4 shorter events, 0.1 us)
Async XLA Ops:
  5.1 2.2 %copy-start = (bf16[16,2,64,1024]{3,2,1,0:T(8,128)(2,1)S(1)}, bf16[16,2,64,1024]{3,2,1,0:T(8,128)(2,1)}, u32[]{:S(2)}) copy-start(bf16[16,2,64,1024]{3,2,1,0:T(8,128)(2,1)} %pool_ref.1) | copy-start | bytes 12582916
  7.3 1.0 %copy-start.1 = (bf16[2,1024,128]{2,1,0:T(8,128)(2,1)S(1)}, bf16[2,1024,128]{2,1,0:T(8,128)(2,1)}, u32[]{:S(2)}) copy-start(bf16[2,1024,128]{2,1,0:T(8,128)(2,1)} %pkv_ref.1) | copy-start | bytes 1572868
  8.4 0.9 copy-start.2
  9.3 0.8 copy-start.3
  10.0 0.7 copy-start.4

commit v2 on v1

v2 whole, which is shorter than its diff:
```python
import functools

import jax
import jax.numpy as jnp
from jax import lax
from jax.experimental import pallas as pl
from jax.experimental.pallas import tpu as pltpu
from jax.sharding import PartitionSpec as P

QUERY_HEADS = 64
KEY_HEADS = 8
HEAD_WIDTH = 128
HEAD_GROUP = QUERY_HEADS // KEY_HEADS
CAP = 4
SIDE = 4
HOMES = SIDE * SIDE

MASK_NEGATIVE = -1e30
EXP2_SCALE = HEAD_WIDTH ** (-0.5) * 1.4426950408889634
FAR_LAST = (1, 3, 2)
SPAN_CHUNK = 256
Z_ROWS = 384


def dot_nt(a, b):
    return lax.dot_general(a, b, (((1,), (1,)), ((), ())), preferred_element_type=jnp.float32)


def dot_nn(a, b):
    return lax.dot_general(a, b, (((1,), (0,)), ((), ())), preferred_element_type=jnp.float32)


def packed_stats(top, total):
    lane = lax.broadcasted_iota(jnp.int32, top.shape, 1)
    return jnp.where(lane < 4, top, total)


def join(stats):
    tops = [s[0:4] for s in stats]
    top = functools.reduce(jnp.maximum, tops)
    weights = [jnp.exp2((t - top) * EXP2_SCALE) * s[4:8] for t, s in zip(tops, stats)]
    total = functools.reduce(jnp.add, weights)
    inverse = 1.0 / jnp.where(total > 0.0, total, 1.0)
    return [w * inverse for w in weights], top, total


def blend(shares, row, parts):
    out = None
    for share, part in zip(shares, parts):
        wide = jnp.broadcast_to(share[row : row + 1], (HEAD_WIDTH, share.shape[1]))
        term = jnp.transpose(wide) * part().astype(jnp.float32)
        out = term if out is None else out + term
    return out


def fused_kernel(
    sq_ref, skv_ref, pkv_ref, start_ref, pool_ref, dest_ref, request_ref, fill_ref, dq_ref, dkv_ref,
    att_ref, dec_ref,
    stage, stage_q, span, qb, kv, kvs, vv, dqb, dkv, pool, acc, mx, col,
    pout, pst, pin, pinst,
    zout, yout, zst, yst, zin, zinst, yin, yinst,
    zb, zbst, zbin, zbinst, yb, ybst, ybin, ybinst,
    own_out, own_st,
    load_sem, q_s, q_r, kv_s, kv_r, ks_s, ks_r, d_s, d_r, f_s, f_r, p_s, p_r,
    za_s, za_r, zs_s, zs_r, ya_s, ya_r, ys_s, ys_r, zb_s, zb_r, yb_s, yb_r,
):
    me = lax.axis_index("seq")
    y, z = me // SIDE, me % SIDE
    rows = sq_ref.shape[0]
    block = KEY_HEADS * rows
    keys = pkv_ref.shape[1]
    mesh_id = pl.DeviceIdType.MESH
    near = (1, 3)

    def at(dy, dz):
        return {"seq": (y + dy) % SIDE * SIDE + (z + dz) % SIDE}

    def remote(src, dst, send, recv, dy, dz):
        return pltpu.make_async_remote_copy(
            src_ref=src, dst_ref=dst, send_sem=send, recv_sem=recv,
            device_id=at(dy, dz), device_id_type=mesh_id,
        )

    sent = []

    def send(*args):
        copy = remote(*args)
        copy.start()
        sent.append(copy)
        return copy

    barrier = pltpu.get_barrier_semaphore()
    for o in (1, 2, 3):
        pl.semaphore_signal(barrier, inc=1, device_id=at(o, 0), device_id_type=mesh_id)
        pl.semaphore_signal(barrier, inc=1, device_id=at(0, o), device_id_type=mesh_id)

    load_prompt = pltpu.make_async_copy(pkv_ref, stage, load_sem.at[0])
    load_dq = pltpu.make_async_copy(dq_ref, dqb.at[0, 0], load_sem.at[1])
    load_span = pltpu.make_async_copy(skv_ref, span, load_sem.at[2])
    load_pool = pltpu.make_async_copy(pool_ref, pool, load_sem.at[3])
    load_dkv = pltpu.make_async_copy(dkv_ref, dkv, load_sem.at[4])
    load_queries = pltpu.make_async_copy(sq_ref, stage_q, load_sem.at[5])
    load_dq.start()
    load_queries.start()
    for c in (load_prompt, load_span, load_pool, load_dkv):
        c.start()

    load_dq.wait()
    load_queries.wait()
    for h in range(KEY_HEADS):
        qb[0, pl.ds(h * rows, rows), :] = stage_q[:, pl.ds(h * HEAD_WIDTH, HEAD_WIDTH)]
    pl.semaphore_wait(barrier, 6)

    q_c, d_c, f_c, kv_c, ks_c = {}, {}, {}, {}, {}
    for o in FAR_LAST:
        q_c[o] = send(qb.at[0], qb.at[o], q_s.at[o], q_r.at[o], o, 0)
        d_c[0, o] = send(dqb.at[0, 0], dqb.at[0, o], d_s.at[0, o], d_r.at[0, o], 0, o)

    def pass_queries(oz):
        for o in near:
            d_c[o, oz] = send(dqb.at[0, oz], dqb.at[o, oz], d_s.at[o, oz], d_r.at[o, oz], o, 0)

    def pass_queries_on(oz):
        for i, o in enumerate(near):
            d_c[o, oz].wait_recv()
            f_c[oz, i] = send(
                dqb.at[o, oz, i], dqb.at[2, oz, i], f_s.at[oz, i], f_r.at[oz, i], o, 0
            )

    pass_queries(0)

    load_prompt.wait()
    start = start_ref[0]
    position = me * keys + lax.broadcasted_iota(jnp.int32, (keys, HEAD_WIDTH), 0)
    own_keys = stage[0].astype(jnp.float32)
    kv[0, 0] = jnp.where(position < start, own_keys, own_keys[0:1]).astype(jnp.bfloat16)
    kv[0, 1] = jnp.where(position < start, stage[1].astype(jnp.float32), 0.0).astype(jnp.bfloat16)
    for first in (0, 1):
        for i, o in enumerate(near):
            c = (first + i) % 2
            kv_c[o, c] = send(kv.at[0, c], kv.at[o, c], kv_s.at[o, c], kv_r.at[o, c], 0, o)
    load_span.wait()
    kvs[0] = span[...]
    for o in FAR_LAST:
        ks_c[o] = send(
            span, kvs.at[o], ks_s.at[o], ks_r.at[o], 0, o
        )

    def pass_shards_on():
        for c, o in enumerate(near):
            kv_c[o, c].wait_recv()
            kv_c[2, c] = send(kv.at[o, c], kv.at[2, c], kv_s.at[2, c], kv_r.at[2, c], 0, o)

    def load_values(oz):
        shard = y * SIDE + (z - oz + SIDE) % SIDE
        position = shard * keys + lax.broadcasted_iota(jnp.int32, (keys, HEAD_WIDTH), 0)
        vv[:, 0:HEAD_WIDTH] = kv[oz, 1]
        vv[:, HEAD_WIDTH:] = jnp.where(position < start, 1.0, 0.0).astype(jnp.bfloat16)

    def prompt_rows(oy, oz, first):
        s = dot_nt(qb[oy], kv[oz, 0])
        top = jnp.broadcast_to(jnp.max(s, axis=1, keepdims=True), (block, HEAD_WIDTH))
        if not first:
            old = mx[oy]
            top = jnp.maximum(old, top)
        wide = jnp.concatenate([top] * (keys // HEAD_WIDTH), axis=1)
        p = jnp.exp2((s - wide) * EXP2_SCALE).astype(jnp.bfloat16)
        o = dot_nn(p, vv[...])
        if not first:
            keep = jnp.exp2((old - top) * EXP2_SCALE)
            o = o + acc[oy] * jnp.concatenate([keep, keep], axis=1)
        acc[oy] = o
        mx[oy] = top

    def prompt_block(oz):
        def step(i, _):
            prompt_rows(2 * i, oz, False)
            prompt_rows(2 * i + 1, oz, False)
            return 0

        lax.fori_loop(0, SIDE // 2, step, 0)

    def span_block(oy):
        width = SIDE * rows
        ones = jnp.ones((width, HEAD_WIDTH), jnp.bfloat16)
        values = jnp.concatenate([jnp.concatenate([kvs[o, 1] for o in range(SIDE)], axis=0), ones], axis=1)
        span_keys = jnp.concatenate([kvs[o, 0] for o in range(SIDE)], axis=0)
        row_base = ((y - oy + SIDE) % SIDE * SIDE + z) * rows

        def step(i, _):
            here = pl.ds(pl.multiple_of(i * SPAN_CHUNK, SPAN_CHUNK), SPAN_CHUNK)
            s = dot_nt(qb[oy, here, :], span_keys)
            row = row_base + lax.broadcasted_iota(jnp.int32, (SPAN_CHUNK, width), 0) % rows
            key = lax.broadcasted_iota(jnp.int32, (SPAN_CHUNK, width), 1)
            key = (y * SIDE + (z - key // rows + SIDE) % SIDE) * rows + key % rows
            valid = key <= row
            s = jnp.where(valid, s, MASK_NEGATIVE)
            old = mx[oy, here, :]
            top = jnp.broadcast_to(jnp.max(s, axis=1, keepdims=True), (SPAN_CHUNK, HEAD_WIDTH))
            top = jnp.maximum(old, top)
            wide = jnp.concatenate([top] * (width // HEAD_WIDTH), axis=1)
            p = jnp.where(valid, jnp.exp2((s - wide) * EXP2_SCALE), 0.0).astype(jnp.bfloat16)
            o = dot_nn(p, values)
            keep = jnp.exp2((old - top) * EXP2_SCALE)
            o = o + acc[oy, here, :] * jnp.concatenate([keep, keep], axis=1)
            total = o[:, HEAD_WIDTH:]
            pout[oy, here, :] = (o[:, :HEAD_WIDTH] / total).astype(jnp.bfloat16)
            col[here, :] = packed_stats(top, total)
            return 0

        lax.fori_loop(0, block // SPAN_CHUNK, step, 0)
        pst[oy] = jnp.transpose(col[...])[0:8]

    pair_rows = block // KEY_HEADS
    tokens = pool.shape[2]
    window = CAP * tokens

    def slots_of(home):
        def scan(b, carry):
            count, found = carry[0], carry[1:]
            hit = dest_ref[b, 0] == home
            found = [jnp.where(hit & (count == c), b, f) for c, f in enumerate(found)]
            return (count + hit.astype(jnp.int32), *found)

        zero = jnp.int32(0)
        count, *found = lax.fori_loop(0, pool.shape[0], scan, (zero,) * (1 + CAP), unroll=4)
        fills = [jnp.where(count > c, fill_ref[f], 0) for c, f in enumerate(found)]
        return found, [request_ref[f] for f in found], fills

    def query_rows(oy, oz, h):
        half = KEY_HEADS // 2
        return dqb[oy, oz, h // half, pl.ds(h % half * pair_rows, pair_rows), :]

    def decode_home(oy, oz):
        home = (y - oy + SIDE) % SIDE * SIDE + (z - oz + SIDE) % SIDE
        index, requests, fills = slots_of(home)
        row = lax.broadcasted_iota(jnp.int32, (pair_rows, window), 0)
        key = lax.broadcasted_iota(jnp.int32, (pair_rows, window), 1)
        which = key // tokens
        request = jnp.zeros((pair_rows, window), jnp.int32)
        fill = jnp.zeros((pair_rows, window), jnp.int32)
        for c in range(CAP):
            request = jnp.where(which == c, requests[c], request)
            fill = jnp.where(which == c, fills[c], fill)
        valid = (row // (pair_rows // 2) == request) & (key % tokens < fill)
        valid_float = jnp.where(valid, 1.0, 0.0)
        ones = jnp.ones((window, HEAD_WIDTH), jnp.bfloat16)

        for h in range(KEY_HEADS):
            lanes = pl.ds(h * HEAD_WIDTH, HEAD_WIDTH)
            here = pl.ds(h * pair_rows, pair_rows)
            k = jnp.concatenate([pool[i, 0, :, lanes] for i in index], axis=0)
            v = jnp.concatenate([pool[i, 1, :, lanes] for i in index], axis=0)
            ok = valid_float > 0.5
            s = jnp.where(ok, dot_nt(query_rows(oy, oz, h), k), MASK_NEGATIVE)
            top = jnp.max(s, axis=1, keepdims=True)
            p = jnp.where(ok, jnp.exp2((s - top) * EXP2_SCALE), 0.0).astype(jnp.bfloat16)
            o = dot_nn(p, jnp.concatenate([v, ones], axis=1))
            total = o[:, HEAD_WIDTH:]
            out = o[:, :HEAD_WIDTH] / jnp.where(total > 0.0, total, 1.0)
            out = out.astype(jnp.bfloat16)
            if h < Z_ROWS // pair_rows:
                zout[oz, oy, here, :] = out
            else:
                yout[oy, oz, pl.ds(h * pair_rows - Z_ROWS, pair_rows), :] = out
            col[here, :] = packed_stats(jnp.broadcast_to(top, total.shape), total)
        stats = jnp.transpose(col[...])[0:8]
        for i in (0, 4):
            zst[oz, i + oy : i + oy + 1, :] = stats[i + oy : i + oy + 1, :Z_ROWS]
            yst[oy, i + oz : i + oz + 1, :] = stats[i + oz : i + oz + 1, Z_ROWS:]

    za_c, zs_c, ya_c, ys_c = {}, {}, {}, {}
    z_part, y_part = pl.ds(0, Z_ROWS), pl.ds(Z_ROWS, block - Z_ROWS)

    def send_partials(oy, oz):
        if oz:
            za_c[oz, oy] = send(
                zout.at[oz, oy], zin.at[oz, oy], za_s.at[oz, oy], za_r.at[oz, oy],
                0, SIDE - oz,
            )
        if oy:
            ya_c[oy, oz] = send(
                yout.at[oy, oz], yin.at[oy, oz], ya_s.at[oy, oz], ya_r.at[oy, oz],
                SIDE - oy, 0,
            )

    def send_z_stats(oz):
        zs_c[oz] = send(zst.at[oz], zinst.at[oz], zs_s.at[oz], zs_r.at[oz], 0, SIDE - oz)

    def send_y_stats(oy):
        ys_c[oy] = send(yst.at[oy], yinst.at[oy], ys_s.at[oy], ys_r.at[oy], SIDE - oy, 0)

    def home(oy, oz):
        decode_home(oy, oz)
        send_partials(oy, oz)

    load_values(0)
    prompt_rows(0, 0, True)
    for oz in FAR_LAST:
        d_c[0, oz].wait_recv()
        pass_queries(oz)
    for oy in FAR_LAST:
        q_c[oy].wait_recv()
        prompt_rows(oy, 0, True)
    load_pool.wait()
    home(0, 0)
    for oz in FAR_LAST:
        home(0, oz)
    pass_queries_on(0)
    home(1, 0)
    home(3, 0)
    pass_shards_on()
    for oz in FAR_LAST:
        pass_queries_on(oz)
        home(1, oz)
        home(3, oz)
        if oz != 2:
            kv_c[oz, oz // 2 ^ 1].wait_recv()
            load_values(oz)
            prompt_block(oz)
    for oz in (1, 3, 2, 0):
        f_c[oz, 0].wait_recv()
        f_c[oz, 1].wait_recv()
        home(2, oz)
    for o in FAR_LAST:
        send_z_stats(o)
        send_y_stats(o)

    kv_c[2, 0].wait_recv()
    kv_c[2, 1].wait_recv()
    load_values(2)
    prompt_block(2)
    for oz in FAR_LAST:
        ks_c[oz].wait_recv()
    p_c = {}
    for oy in (2, 1, 3, 0):
        span_block(oy)
        if oy:
            p_c[oy, 0] = send(pout.at[oy], pin.at[oy], p_s.at[oy, 0], p_r.at[oy, 0], SIDE - oy, 0)
            p_c[oy, 1] = send(
                pst.at[oy], pinst.at[oy], p_s.at[oy, 1], p_r.at[oy, 1], SIDE - oy, 0
            )

    load_dkv.wait()
    extra = dkv.shape[2]
    row = lax.broadcasted_iota(jnp.int32, (pair_rows, extra), 0)
    key = lax.broadcasted_iota(jnp.int32, (pair_rows, extra), 1)
    step_of_row = row % (pair_rows // 2) // HEAD_GROUP
    fresh = (row // (pair_rows // 2) == key // (extra // 2)) & (key % (extra // 2) <= step_of_row)
    ones = jnp.ones((extra, HEAD_WIDTH), jnp.bfloat16)
    for h in range(KEY_HEADS):
        here = pl.ds(h * pair_rows, pair_rows)
        s = jnp.where(fresh, dot_nt(query_rows(0, 0, h), dkv[0, h]), MASK_NEGATIVE)
        top = jnp.max(s, axis=1, keepdims=True)
        p = jnp.where(fresh, jnp.exp2((s - top) * EXP2_SCALE), 0.0).astype(jnp.bfloat16)
        o = dot_nn(p, jnp.concatenate([dkv[1, h], ones], axis=1))
        total = o[:, HEAD_WIDTH:]
        own_out[here, :] = o[:, :HEAD_WIDTH] / total
        col[here, :] = packed_stats(jnp.broadcast_to(top, total.shape), total)
    own_st[...] = jnp.transpose(col[...])[0:8]

    def spread(top, total, row):
        shape = (8, top.shape[1])
        sub = lax.broadcasted_iota(jnp.int32, shape, 0)
        return jnp.where(
            sub < 4,
            jnp.broadcast_to(top[row : row + 1], shape),
            jnp.broadcast_to(total[row : row + 1], shape),
        )

    zb_c, yb_c = {}, {}
    for oz in FAR_LAST:
        zs_c[oz].wait_recv()
    shares, top, total = join([zst[0]] + [zinst[oz] for oz in FAR_LAST])
    for oy in (1, 3, 2, 0):
        for oz in FAR_LAST:
            za_c[oz, oy].wait_recv()
        out = blend(
            shares, oy,
            [lambda oy=oy: zout[0, oy]]
            + [lambda oz=oz, oy=oy: zin[oz, oy] for oz in FAR_LAST],
        )
        zb[oy] = out.astype(jnp.bfloat16)
        zbst[oy] = spread(top, total, oy)
        if oy:
            zb_c[oy, 0] = send(zb.at[oy], zbin.at[oy], zb_s.at[oy, 0], zb_r.at[oy, 0], SIDE - oy, 0)
            zb_c[oy, 1] = send(
                zbst.at[oy], zbinst.at[oy], zb_s.at[oy, 1], zb_r.at[oy, 1], SIDE - oy, 0
            )
    for oy in FAR_LAST:
        ys_c[oy].wait_recv()
    shares, top, total = join([yst[0]] + [yinst[oy] for oy in FAR_LAST])
    for oz in (1, 3, 2, 0):
        for oy in FAR_LAST:
            ya_c[oy, oz].wait_recv()
        out = blend(
            shares, oz,
            [lambda oz=oz: yout[0, oz]]
            + [lambda oz=oz, oy=oy: yin[oy, oz] for oy in FAR_LAST],
        )
        yb[oz] = out.astype(jnp.bfloat16)
        ybst[oz] = spread(top, total, oz)
        if oz:
            yb_c[oz, 0] = send(yb.at[oz], ybin.at[oz], yb_s.at[oz, 0], yb_r.at[oz, 0], 0, SIDE - oz)
            yb_c[oz, 1] = send(
                ybst.at[oz], ybinst.at[oz], yb_s.at[oz, 1], yb_r.at[oz, 1], 0, SIDE - oz
            )

    for oy in FAR_LAST:
        p_c[oy, 0].wait_recv()
        p_c[oy, 1].wait_recv()
    shares, _, _ = join([pst[0]] + [pinst[oy] for oy in FAR_LAST])
    out = blend(shares, 0, [lambda: pout[0]] + [lambda oy=oy: pin[oy] for oy in FAR_LAST])
    out = out.astype(jnp.bfloat16)
    for h in range(KEY_HEADS):
        att_ref[:, pl.ds(h * HEAD_WIDTH, HEAD_WIDTH)] = out[h * rows : (h + 1) * rows]

    for c in list(zb_c.values()) + list(yb_c.values()):
        c.wait_recv()
    for part, n, part_out, part_st, into, into_st in (
        (z_part, Z_ROWS, zb, zbst, zbin, zbinst),
        (y_part, block - Z_ROWS, yb, ybst, ybin, ybinst),
    ):
        shares, _, _ = join(
            [own_st[:, part], part_st[0]] + [into_st[o] for o in FAR_LAST]
        )
        out = blend(
            shares, 0,
            [lambda part=part: own_out[part, :], lambda part_out=part_out: part_out[0]]
            + [lambda o=o, into=into: into[o] for o in FAR_LAST],
        )
        dec_ref[part, :] = out.astype(jnp.bfloat16)

    for c in sent:
        c.wait_send()


def on_device(
    span_queries,
    span_key_value,
    prompt_key_value,
    span_start,
    block_pool_key_value,
    block_dest,
    block_request,
    block_fill,
    decode_query,
    decoded_key_value,
):
    steps, requests = decode_query.shape[:2]
    rows = span_queries.shape[0]
    block = KEY_HEADS * rows
    keys = prompt_key_value.shape[1]
    dq = decode_query.reshape(steps, requests, KEY_HEADS, HEAD_GROUP, HEAD_WIDTH)
    dq = dq.transpose(2, 1, 0, 3, 4).reshape(2, block // 2, HEAD_WIDTH)
    dkv = decoded_key_value.reshape(steps, 2, requests, KEY_HEADS, HEAD_WIDTH)
    dkv = dkv.transpose(1, 3, 2, 0, 4)
    dkv = jnp.pad(dkv, ((0, 0), (0, 0), (0, 0), (0, 8 - steps), (0, 0)))
    dkv = dkv.reshape(2, KEY_HEADS, 8 * requests, HEAD_WIDTH)

    bf, f32 = jnp.bfloat16, jnp.float32
    part = (block, HEAD_WIDTH)
    z_part, y_part = (Z_ROWS, HEAD_WIDTH), (block - Z_ROWS, HEAD_WIDTH)
    stat, z_stat, y_stat = (8, block), (8, Z_ROWS), (8, block - Z_ROWS)
    vmem = pl.BlockSpec(memory_space=pltpu.VMEM)
    smem = pl.BlockSpec(memory_space=pltpu.SMEM)
    hbm = pl.BlockSpec(memory_space=pl.ANY)
    dma = pltpu.SemaphoreType.DMA
    one, two = (SIDE,), (SIDE, SIDE)
    buffers = [
        ((2, keys, HEAD_WIDTH), bf),
        (span_queries.shape, bf),
        ((2, rows, HEAD_WIDTH), bf),
        (one + part, bf),
        ((SIDE, 2, keys, HEAD_WIDTH), bf),
        ((SIDE, 2, rows, HEAD_WIDTH), bf),
        ((keys, 2 * HEAD_WIDTH), bf),
        (two + dq.shape, bf),
        (dkv.shape, bf),
        (block_pool_key_value.shape, bf),
        ((SIDE, block, 2 * HEAD_WIDTH), f32),
        (one + part, f32),
        (part, f32),
        (one + part, bf), (one + stat, f32),
        (one + part, bf), (one + stat, f32),
        (two + z_part, bf), (two + y_part, bf),
        (one + z_stat, f32), (one + y_stat, f32),
        (two + z_part, bf), (one + z_stat, f32),
        (two + y_part, bf), (one + y_stat, f32),
        (one + z_part, bf), (one + z_stat, f32),
        (one + z_part, bf), (one + z_stat, f32),
        (one + y_part, bf), (one + y_stat, f32),
        (one + y_part, bf), (one + y_stat, f32),
        (part, f32), (stat, f32),
    ]
    pairs = [one, (SIDE, 2), one, two, (SIDE, 2), (SIDE, 2), two, one, two, one, (SIDE, 2), (SIDE, 2)]
    semaphores = [dma((6,))]
    for shape in pairs:
        semaphores += [dma(shape), dma(shape)]
    attended, dec = pl.pallas_call(
        fused_kernel,
        out_shape=(
            jax.ShapeDtypeStruct(span_queries.shape, bf),
            jax.ShapeDtypeStruct(part, bf),
        ),
        in_specs=[hbm, hbm, hbm, smem, hbm, smem, smem, smem, hbm, hbm],
        out_specs=(vmem, vmem),
        scratch_shapes=[pltpu.VMEM(shape, dtype) for shape, dtype in buffers] + semaphores,
        compiler_params=pltpu.CompilerParams(
            collective_id=0, has_side_effects=True, vmem_limit_bytes=48 * 1024 * 1024
        ),
        name="span_and_decode",
    )(span_queries, span_key_value, prompt_key_value, span_start, block_pool_key_value, block_dest,
      block_request, block_fill, dq, dkv)
    dec = dec.reshape(KEY_HEADS, requests, steps, HEAD_GROUP, HEAD_WIDTH)
    dec = dec.transpose(2, 1, 0, 3, 4).reshape(steps, requests, QUERY_HEADS * HEAD_WIDTH)
    return attended, dec


def solution(mesh):
    placed = (
        P("seq", "req"),
        P(None, "seq", "req"),
        P(None, "seq", "req"),
        P(),
        P(("seq", "req"), None, None, None),
        P(("seq", "req"), None),
        P(("seq", "req")),
        P(("seq", "req")),
        P(None, ("seq", "req"), None),
        P(None, None, ("seq", "req"), None),
    )
    return jax.shard_map(
        on_device,
        mesh=mesh,
        in_specs=placed,
        out_specs=(P("seq", "req"), P(None, ("seq", "req"), None)),
        check_vma=False,
    )
```

time: 99.9 us -> 72.3 us (0.72)
  Pallas kernels: 89.3 us -> 60.4 us
  local copies, waits for them, and re-layouts: 8.8 us -> 10.2 us
    pallas_call x1, Pallas kernels: 87.4 us -> 60.4 us  [on_device(): pl.pallas_call(fused_kernel, out_shape=(jax.ShapeDtypeStruct(span_queries...]
    pallas_call x1 -> x0, Pallas kernels: 1.95 us -> none  [block_slots(): pl.pallas_call(slots_kernel, out_shape=jax.ShapeDtypeStruct((3 * HOMES *...]
    unnamed x11 -> x14, local copies, waits for them, and re-layouts: 6.22 us -> 7.58 us
where the time goes in v2:
time: 72.3 us; the launch traced here: 71.9 us
  Pallas kernels  60.4 us (84%)
  local copies, waits for them, and re-layouts  10.2 us (14%)
  between operations  1.33 us (2%)
    pallas_call x1, Pallas kernels, on_device(): pl.pallas_call(fused_kernel, out_shape=(jax.ShapeDtypeStruct(span_queries...  60.4 us
    unnamed x14, local copies, waits for them, and re-layouts  7.58 us

profile of v2, /device:TPU:0, one launch (start us, length us, event | category | flops | bytes accessed | tf_op | source)
XLA Modules:
  0.0 71.9 jit_solution(17972740301999999247)
XLA Ops:
  1.3 0.7 %copy.14.dest_ref = s32[16,1]{1,0:T(8,128)S(1)} copy(s32[16,1]{0,1:T(1,128)} %param.15) | data formatting | bytes 128 | tf_op args[5]
  2.0 0.8 %reshape.24 = bf16[4,2,2,8,128]{4,3,2,1,0:T(8,128)(2,1)S(1)} reshape(bf16[4,2,2,1024]{3,2,1,0:T(2,128)(2,1)} %param.19) | data formatting | bytes 65536 | tf_op jit(solution)/shard_map/reshape | solution.py:456
  2.8 1.0 %reshape.22 = bf16[4,2,8,8,128]{4,3,2,1,0:T(8,128)(2,1)S(1)} reshape(bf16[4,2,8192]{2,1,0:T(2,128)(2,1)} %param.18) | data formatting | bytes 262144 | tf_op jit(solution)/shard_map/reshape | solution.py:454
  3.9 0.0 copy-start
  3.9 2.2 %copy-done = bf16[16,2,64,1024]{3,2,1,0:T(8,128)(2,1)S(1)} copy-done((bf16[16,2,64,1024]{3,2,1,0:T(8,128)(2,1)S(1)}, bf16[16,2,64,1024]{3,2,1,0:T(8,128)(2,1)}, u32[]{:S(2)}) %copy-start) | copy-done | bytes 4194328
  6.1 0.0 copy-start.1
  6.1 1.0 %copy-done.1 = bf16[2,1024,128]{2,1,0:T(8,128)(2,1)S(1)} copy-done((bf16[2,1024,128]{2,1,0:T(8,128)(2,1)S(1)}, bf16[2,1024,128]{2,1,0:T(8,128)(2,1)}, u32[]{:S(2)}) %copy-start.1) | copy-done | bytes 524312
  7.1 0.0 copy-start.2
  7.1 0.9 %copy-done.2 = bf16[64,1024]{1,0:T(8,128)(2,1)S(1)} copy-done((bf16[64,1024]{1,0:T(8,128)(2,1)S(1)}, bf16[64,1024]{1,0:T(8,128)(2,1)}, u32[]{:S(2)}) %copy-start.2) | copy-done | bytes 131096
  8.0 0.0 copy-start.3
  8.0 0.8 %copy-done.3 = bf16[2,64,128]{2,1,0:T(8,128)(2,1)S(1)} copy-done((bf16[2,64,128]{2,1,0:T(8,128)(2,1)S(1)}, bf16[2,64,128]{2,1,0:T(8,128)(2,1)}, u32[]{:S(2)}) %copy-start.3) | copy-done | bytes 32792
  8.8 0.0 copy-start.4
  8.8 0.7 copy-done.4
  9.4 0.0 copy-start.5
  9.4 0.7 copy-done.5
  10.1 60.4 %span_and_decode.1 = (bf16[64,1024]{1,0:T(8,128)(2,1)S(1)}, bf16[512,128]{1,0:T(8,128)(2,1)S(1)}) custom-call(bf16[64,1024]{1,0:T(8,128)(2,1)S(1)} %copy-done.2, bf16[2,64,128]{2,1,0:T(8,128)(2,1)S(1)} %copy-done.3, bf16[2,1024,128]{2,1,0:T(8,128)(2,1)S(1)} %copy-done.1, s32[1]{0:T(128)S(6)} %copy.19.start_ref, bf16[16,2,64,1024]{3,2,1,0:T(8,128)(2,1)S(1)} %copy-done, ...), custom_call_target="tpu_custom_call" | custom-call | tf_op jit(solution)/shard_map/span_and_decode/pallas_call | solution.py:500
  70.6 0.7 reshape.27
  71.3 0.7 copy.20
  (4 shorter events, 0.1 us)
Async XLA Ops:
  3.9 2.2 %copy-start = (bf16[16,2,64,1024]{3,2,1,0:T(8,128)(2,1)S(1)}, bf16[16,2,64,1024]{3,2,1,0:T(8,128)(2,1)}, u32[]{:S(2)}) copy-start(bf16[16,2,64,1024]{3,2,1,0:T(8,128)(2,1)} %pool_ref.1) | copy-start | bytes 12582916
  6.1 1.0 %copy-start.1 = (bf16[2,1024,128]{2,1,0:T(8,128)(2,1)S(1)}, bf16[2,1024,128]{2,1,0:T(8,128)(2,1)}, u32[]{:S(2)}) copy-start(bf16[2,1024,128]{2,1,0:T(8,128)(2,1)} %pkv_ref.1) | copy-start | bytes 1572868
  7.1 0.9 %copy-start.2 = (bf16[64,1024]{1,0:T(8,128)(2,1)S(1)}, bf16[64,1024]{1,0:T(8,128)(2,1)}, u32[]{:S(2)}) copy-start(bf16[64,1024]{1,0:T(8,128)(2,1)} %sq_ref.1) | copy-start | bytes 393220
  8.0 0.8 %copy-start.3 = (bf16[2,64,128]{2,1,0:T(8,128)(2,1)S(1)}, bf16[2,64,128]{2,1,0:T(8,128)(2,1)}, u32[]{:S(2)}) copy-start(bf16[2,64,128]{2,1,0:T(8,128)(2,1)} %skv_ref.1) | copy-start | bytes 98308
  8.8 0.7 copy-start.4
  9.4 0.7 copy-start.5

commit v3 on v2

--- a/solution.py
+++ b/solution.py
@@ -56,7 +56,7 @@
 def fused_kernel(
     sq_ref, skv_ref, pkv_ref, start_ref, pool_ref, dest_ref, request_ref, fill_ref, dq_ref, dkv_ref,
     att_ref, dec_ref,
-    stage, stage_q, span, qb, kv, kvs, vv, dqb, dkv, pool, acc, mx, col,
+    stage, stage_q, span, qb, kv, kvs, vv, dqb, stage_d, dkv, pool, acc, mx, col,
     pout, pst, pin, pinst,
     zout, yout, zst, yst, zin, zinst, yin, yinst,
     zb, zbst, zbin, zbinst, yb, ybst, ybin, ybinst,
@@ -98,7 +98,7 @@
     load_dq = pltpu.make_async_copy(dq_ref, dqb.at[0, 0], load_sem.at[1])
     load_span = pltpu.make_async_copy(skv_ref, span, load_sem.at[2])
     load_pool = pltpu.make_async_copy(pool_ref, pool, load_sem.at[3])
-    load_dkv = pltpu.make_async_copy(dkv_ref, dkv, load_sem.at[4])
+    load_dkv = pltpu.make_async_copy(dkv_ref, stage_d, load_sem.at[4])
     load_queries = pltpu.make_async_copy(sq_ref, stage_q, load_sem.at[5])
     load_dq.start()
     load_queries.start()
@@ -108,7 +108,7 @@
     load_dq.wait()
     load_queries.wait()
     for h in range(KEY_HEADS):
-        qb[0, pl.ds(h * rows, rows), :] = stage_q[:, pl.ds(h * HEAD_WIDTH, HEAD_WIDTH)]
+        qb[0, h // 4, pl.ds(h % 4 * rows, rows), :] = stage_q[:, pl.ds(h * HEAD_WIDTH, HEAD_WIDTH)]
     pl.semaphore_wait(barrier, 6)
 
     q_c, d_c, f_c, kv_c, ks_c = {}, {}, {}, {}, {}
@@ -158,7 +158,7 @@
         vv[:, HEAD_WIDTH:] = jnp.where(position < start, 1.0, 0.0).astype(jnp.bfloat16)
 
     def prompt_rows(oy, oz, first):
-        s = dot_nt(qb[oy], kv[oz, 0])
+        s = dot_nt(qb[oy].reshape(block, HEAD_WIDTH), kv[oz, 0])
         top = jnp.broadcast_to(jnp.max(s, axis=1, keepdims=True), (block, HEAD_WIDTH))
         if not first:
             old = mx[oy]
@@ -189,7 +189,7 @@
 
         def step(i, _):
             here = pl.ds(pl.multiple_of(i * SPAN_CHUNK, SPAN_CHUNK), SPAN_CHUNK)
-            s = dot_nt(qb[oy, here, :], span_keys)
+            s = dot_nt(qb[oy, i], span_keys)
             row = row_base + lax.broadcasted_iota(jnp.int32, (SPAN_CHUNK, width), 0) % rows
             key = lax.broadcasted_iota(jnp.int32, (SPAN_CHUNK, width), 1)
             key = (y * SIDE + (z - key // rows + SIDE) % SIDE) * rows + key % rows
@@ -218,7 +218,7 @@
     def slots_of(home):
         def scan(b, carry):
             count, found = carry[0], carry[1:]
-            hit = dest_ref[b, 0] == home
+            hit = dest_ref[b] == home
             found = [jnp.where(hit & (count == c), b, f) for c, f in enumerate(found)]
             return (count + hit.astype(jnp.int32), *found)
 
@@ -342,18 +342,27 @@
             )
 
     load_dkv.wait()
+    steps, _, requests, _ = stage_d.shape
+    dkv[...] = jnp.zeros_like(dkv)
+    for u in range(steps):
+        for c in range(2):
+            new = stage_d[u, c].astype(jnp.float32)
+            for h in range(KEY_HEADS):
+                dkv[c, h, pl.ds(u * requests, requests), :] = new[
+                    :, h * HEAD_WIDTH : (h + 1) * HEAD_WIDTH
+                ]
     extra = dkv.shape[2]
     row = lax.broadcasted_iota(jnp.int32, (pair_rows, extra), 0)
     key = lax.broadcasted_iota(jnp.int32, (pair_rows, extra), 1)
     step_of_row = row % (pair_rows // 2) // HEAD_GROUP
-    fresh = (row // (pair_rows // 2) == key // (extra // 2)) & (key % (extra // 2) <= step_of_row)
+    fresh = (row // (pair_rows // 2) == key % requests) & (key // requests <= step_of_row)
     ones = jnp.ones((extra, HEAD_WIDTH), jnp.bfloat16)
     for h in range(KEY_HEADS):
         here = pl.ds(h * pair_rows, pair_rows)
-        s = jnp.where(fresh, dot_nt(query_rows(0, 0, h), dkv[0, h]), MASK_NEGATIVE)
+        s = jnp.where(fresh, dot_nt(query_rows(0, 0, h), dkv[0, h].astype(jnp.bfloat16)), MASK_NEGATIVE)
         top = jnp.max(s, axis=1, keepdims=True)
         p = jnp.where(fresh, jnp.exp2((s - top) * EXP2_SCALE), 0.0).astype(jnp.bfloat16)
-        o = dot_nn(p, jnp.concatenate([dkv[1, h], ones], axis=1))
+        o = dot_nn(p, jnp.concatenate([dkv[1, h].astype(jnp.bfloat16), ones], axis=1))
         total = o[:, HEAD_WIDTH:]
         own_out[here, :] = o[:, :HEAD_WIDTH] / total
         col[here, :] = packed_stats(jnp.broadcast_to(top, total.shape), total)
@@ -453,10 +462,7 @@
     keys = prompt_key_value.shape[1]
     dq = decode_query.reshape(steps, requests, KEY_HEADS, HEAD_GROUP, HEAD_WIDTH)
     dq = dq.transpose(2, 1, 0, 3, 4).reshape(2, block // 2, HEAD_WIDTH)
-    dkv = decoded_key_value.reshape(steps, 2, requests, KEY_HEADS, HEAD_WIDTH)
-    dkv = dkv.transpose(1, 3, 2, 0, 4)
-    dkv = jnp.pad(dkv, ((0, 0), (0, 0), (0, 0), (0, 8 - steps), (0, 0)))
-    dkv = dkv.reshape(2, KEY_HEADS, 8 * requests, HEAD_WIDTH)
+    decoded = decoded_key_value.shape
 
     bf, f32 = jnp.bfloat16, jnp.float32
     part = (block, HEAD_WIDTH)
@@ -464,19 +470,19 @@
     stat, z_stat, y_stat = (8, block), (8, Z_ROWS), (8, block - Z_ROWS)
     vmem = pl.BlockSpec(memory_space=pltpu.VMEM)
     smem = pl.BlockSpec(memory_space=pltpu.SMEM)
-    hbm = pl.BlockSpec(memory_space=pl.ANY)
+    hbm = pl.BlockSpec(memory_space=pltpu.HBM)
     dma = pltpu.SemaphoreType.DMA
     one, two = (SIDE,), (SIDE, SIDE)
     buffers = [
         ((2, keys, HEAD_WIDTH), bf),
         (span_queries.shape, bf),
         ((2, rows, HEAD_WIDTH), bf),
-        (one + part, bf),
+        (one + dq.shape, bf),
         ((SIDE, 2, keys, HEAD_WIDTH), bf),
         ((SIDE, 2, rows, HEAD_WIDTH), bf),
         ((keys, 2 * HEAD_WIDTH), bf),
         (two + dq.shape, bf),
-        (dkv.shape, bf),
+        (decoded, bf), ((2, KEY_HEADS, 2 * steps * requests, HEAD_WIDTH), f32),
         (block_pool_key_value.shape, bf),
         ((SIDE, block, 2 * HEAD_WIDTH), f32),
         (one + part, f32),
@@ -507,11 +513,11 @@
         out_specs=(vmem, vmem),
         scratch_shapes=[pltpu.VMEM(shape, dtype) for shape, dtype in buffers] + semaphores,
         compiler_params=pltpu.CompilerParams(
-            collective_id=0, has_side_effects=True, vmem_limit_bytes=48 * 1024 * 1024
+            collective_id=0, has_side_effects=True, vmem_limit_bytes=64 * 1024 * 1024 - 65536
         ),
         name="span_and_decode",
-    )(span_queries, span_key_value, prompt_key_value, span_start, block_pool_key_value, block_dest,
-      block_request, block_fill, dq, dkv)
+    )(span_queries, span_key_value, prompt_key_value, span_start, block_pool_key_value, block_dest[:, 0],
+      block_request, block_fill, dq, decoded_key_value)
     dec = dec.reshape(KEY_HEADS, requests, steps, HEAD_GROUP, HEAD_WIDTH)
     dec = dec.transpose(2, 1, 0, 3, 4).reshape(steps, requests, QUERY_HEADS * HEAD_WIDTH)
     return attended, dec

time: 72.3 us -> 67.4 us (0.932)
  local copies, waits for them, and re-layouts: 10.2 us -> 4.88 us
    unnamed x14 -> x1, local copies, waits for them, and re-layouts: 7.58 us -> 1.57 us
    transpose x1, local copies, waits for them, and re-layouts: 0.02 us -> 0.93 us  [on_device(): dec.transpose(2, 1, 0, 3, 4)]
    reshape x3 -> x0, local copies, waits for them, and re-layouts: 0.82 us -> none  [the longest x2 0.8 us: on_device(): dkv = decoded_key_value.reshape(steps, 2, requests, KEY_HEADS, HEAD_WIDTH)]
where the time goes in v3:
time: 67.4 us; the launch traced here: 67.2 us
  Pallas kernels  61.1 us (91%)
  local copies, waits for them, and re-layouts  4.88 us (7%)
  between operations  1.29 us (2%)
    pallas_call x1, Pallas kernels, on_device(): pl.pallas_call(fused_kernel, out_shape=(jax.ShapeDtypeStruct(span_queries...  61.1 us
    reshape x2, local copies, waits for them, and re-layouts, on_device(): decode_query.reshape(steps, requests, KEY_HEADS, HEAD_GROUP, HEAD_WIDTH)  1.7 us
    unnamed x1, local copies, waits for them, and re-layouts  1.57 us

profile of v3, /device:TPU:0, one launch (start us, length us, event | category | flops | bytes accessed | tf_op | source)
XLA Modules:
  0.0 67.2 jit_solution(8201882237697513124)
XLA Ops:
  1.3 1.0 %reshape.16 = bf16[4,2,8,8,128]{4,3,2,1,0:T(8,128)(2,1)S(1)} reshape(bf16[4,2,8192]{2,1,0:T(2,128)(2,1)} %param.18) | data formatting | bytes 262144 | tf_op jit(solution)/shard_map/reshape | solution.py:463
  2.3 0.7 %copy.12 = bf16[4,2,8,8,128]{4,3,0,1,2:T(8,128)(2,1)} copy(bf16[4,2,8,8,128]{4,3,2,1,0:T(8,128)(2,1)S(1)} %reshape.16) | data formatting | bytes 262144 | tf_op jit(solution)/shard_map/reshape | solution.py:463
  3.0 61.1 %span_and_decode.1 = (bf16[64,1024]{1,0:T(8,128)(2,1)}, bf16[512,128]{1,0:T(8,128)(2,1)}) custom-call(bf16[64,1024]{1,0:T(8,128)(2,1)} %sq_ref.1, bf16[2,64,128]{2,1,0:T(8,128)(2,1)} %skv_ref.1, bf16[2,1024,128]{2,1,0:T(8,128)(2,1)} %pkv_ref.1, s32[1]{0:T(128)S(6)} %copy.15.start_ref, bf16[16,2,64,1024]{3,2,1,0:T(8,128)(2,1)} %pool_ref.1, s32[16]{0:T(128)} %bitcast.11, ...), custom_call_target="tpu_custom_call" | custom-call | tf_op jit(solution)/shard_map/span_and_decode/pallas_call | solution.py:506
  64.0 0.9 %copy.13 = bf16[4,2,8,8,128]{4,3,2,1,0:T(8,128)(2,1)S(1)} copy(bf16[4,2,8,8,128]{4,3,0,1,2:T(8,128)(2,1)} %bitcast.10) | data formatting | bytes 262144 | tf_op jit(solution)/shard_map/transpose | solution.py:522
  65.0 0.7 %reshape.19 = bf16[4,2,8192]{2,1,0:T(2,128)(2,1)} reshape(bf16[4,2,8,8,128]{4,3,2,1,0:T(8,128)(2,1)S(1)} %copy.13) | data formatting | bytes 262144 | tf_op jit(solution)/shard_map/reshape | solution.py:522
  65.7 1.6 %copy.16 = bf16[64,1024]{1,0:T(8,128)(2,1)} copy(bf16[64,1024]{1,0:T(8,128)(2,1)} %get-tuple-element.8) | data formatting | bytes 262144

commit v4 on v3

--- a/solution.py
+++ b/solution.py
@@ -56,13 +56,13 @@
 def fused_kernel(
     sq_ref, skv_ref, pkv_ref, start_ref, pool_ref, dest_ref, request_ref, fill_ref, dq_ref, dkv_ref,
     att_ref, dec_ref,
-    stage, stage_q, span, qb, kv, kvs, vv, dqb, stage_d, dkv, pool, acc, mx, col,
+    stage, stage_q, span, qb, kv, kvs, vv, dqb, stage_d, stage_dq, dkv, pool, acc, mx, col,
     pout, pst, pin, pinst,
-    zout, yout, zst, yst, zin, zinst, yin, yinst,
+    zout, yout, zst, zfst, yst, zin, zinst, zfinst, yin, yinst,
     zb, zbst, zbin, zbinst, yb, ybst, ybin, ybinst,
-    own_out, own_st,
+    own_out, own_st, perm,
     load_sem, q_s, q_r, kv_s, kv_r, ks_s, ks_r, d_s, d_r, f_s, f_r, p_s, p_r,
-    za_s, za_r, zs_s, zs_r, ya_s, ya_r, ys_s, ys_r, zb_s, zb_r, yb_s, yb_r,
+    za_s, za_r, zs_s, zs_r, zf_s, zf_r, ya_s, ya_r, ys_s, ys_r, zb_s, zb_r, yb_s, yb_r,
 ):
     me = lax.axis_index("seq")
     y, z = me // SIDE, me % SIDE
@@ -95,7 +95,7 @@
         pl.semaphore_signal(barrier, inc=1, device_id=at(0, o), device_id_type=mesh_id)
 
     load_prompt = pltpu.make_async_copy(pkv_ref, stage, load_sem.at[0])
-    load_dq = pltpu.make_async_copy(dq_ref, dqb.at[0, 0], load_sem.at[1])
+    load_dq = pltpu.make_async_copy(dq_ref, stage_dq, load_sem.at[1])
     load_span = pltpu.make_async_copy(skv_ref, span, load_sem.at[2])
     load_pool = pltpu.make_async_copy(pool_ref, pool, load_sem.at[3])
     load_dkv = pltpu.make_async_copy(dkv_ref, stage_d, load_sem.at[4])
@@ -106,6 +106,14 @@
         c.start()
 
     load_dq.wait()
+    for t in range(dq_ref.shape[0]):
+        wide = stage_dq[t].astype(jnp.float32)
+        for n in range(QUERY_HEADS):
+            first = n // HEAD_GROUP * rows + t * HEAD_GROUP + n % HEAD_GROUP
+            perm[pl.ds(first, dq_ref.shape[1], stride=rows // 2), :] = wide[
+                :, n * HEAD_WIDTH : (n + 1) * HEAD_WIDTH
+            ]
+    dqb[0, 0] = perm[0:block, :].astype(jnp.bfloat16).reshape(dqb.shape[2:])
     load_queries.wait()
     for h in range(KEY_HEADS):
         qb[0, h // 4, pl.ds(h % 4 * rows, rows), :] = stage_q[:, pl.ds(h * HEAD_WIDTH, HEAD_WIDTH)]
@@ -265,11 +273,16 @@
                 yout[oy, oz, pl.ds(h * pair_rows - Z_ROWS, pair_rows), :] = out
             col[here, :] = packed_stats(jnp.broadcast_to(top, total.shape), total)
         stats = jnp.transpose(col[...])[0:8]
+        if oy == 2:
+            zfst[oz] = stats[:, :Z_ROWS]
+        elif oy == 0:
+            zst[oz] = stats[:, :Z_ROWS]
         for i in (0, 4):
-            zst[oz, i + oy : i + oy + 1, :] = stats[i + oy : i + oy + 1, :Z_ROWS]
+            if oy % 2:
+                zst[oz, i + oy : i + oy + 1, :] = stats[i + oy : i + oy + 1, :Z_ROWS]
             yst[oy, i + oz : i + oz + 1, :] = stats[i + oz : i + oz + 1, Z_ROWS:]
 
-    za_c, zs_c, ya_c, ys_c = {}, {}, {}, {}
+    za_c, zs_c, zf_c, ya_c, ys_c = {}, {}, {}, {}, {}
     z_part, y_part = pl.ds(0, Z_ROWS), pl.ds(Z_ROWS, block - Z_ROWS)
 
     def send_partials(oy, oz):
@@ -286,6 +299,9 @@
 
     def send_z_stats(oz):
         zs_c[oz] = send(zst.at[oz], zinst.at[oz], zs_s.at[oz], zs_r.at[oz], 0, SIDE - oz)
+
+    def send_far_stats(oz):
+        zf_c[oz] = send(zfst.at[oz], zfinst.at[oz], zf_s.at[oz], zf_r.at[oz], 0, SIDE - oz)
 
     def send_y_stats(oy):
         ys_c[oy] = send(yst.at[oy], yinst.at[oy], ys_s.at[oy], ys_r.at[oy], SIDE - oy, 0)
@@ -318,12 +334,14 @@
             kv_c[oz, oz // 2 ^ 1].wait_recv()
             load_values(oz)
             prompt_block(oz)
+    for o in FAR_LAST:
+        send_z_stats(o)
     for oz in (1, 3, 2, 0):
         f_c[oz, 0].wait_recv()
         f_c[oz, 1].wait_recv()
         home(2, oz)
     for o in FAR_LAST:
-        send_z_stats(o)
+        send_far_stats(o)
         send_y_stats(o)
 
     kv_c[2, 0].wait_recv()
@@ -381,7 +399,11 @@
     for oz in FAR_LAST:
         zs_c[oz].wait_recv()
     shares, top, total = join([zst[0]] + [zinst[oz] for oz in FAR_LAST])
-    for oy in (1, 3, 2, 0):
+    for oy in (1, 3, 0, 2):
+        if oy == 2:
+            for oz in FAR_LAST:
+                zf_c[oz].wait_recv()
+            shares, top, total = join([zfst[0]] + [zfinst[oz] for oz in FAR_LAST])
         for oz in FAR_LAST:
             za_c[oz, oy].wait_recv()
         out = blend(
@@ -438,7 +460,17 @@
             [lambda part=part: own_out[part, :], lambda part_out=part_out: part_out[0]]
             + [lambda o=o, into=into: into[o] for o in FAR_LAST],
         )
-        dec_ref[part, :] = out.astype(jnp.bfloat16)
+        perm[part, :] = out
+
+    half_pair = pair_rows // 2
+    for t in range(steps):
+        for h in range(KEY_HEADS):
+            pieces = [
+                perm[pl.ds(h * pair_rows + t * HEAD_GROUP + g, requests, stride=half_pair), :]
+                for g in range(HEAD_GROUP)
+            ]
+            lanes = pl.ds(h * HEAD_GROUP * HEAD_WIDTH, HEAD_GROUP * HEAD_WIDTH)
+            dec_ref[t, :, lanes] = jnp.concatenate(pieces, axis=1).astype(jnp.bfloat16)
 
     for c in sent:
         c.wait_send()
@@ -460,8 +492,7 @@
     rows = span_queries.shape[0]
     block = KEY_HEADS * rows
     keys = prompt_key_value.shape[1]
-    dq = decode_query.reshape(steps, requests, KEY_HEADS, HEAD_GROUP, HEAD_WIDTH)
-    dq = dq.transpose(2, 1, 0, 3, 4).reshape(2, block // 2, HEAD_WIDTH)
+    halves = (2, block // 2, HEAD_WIDTH)
     decoded = decoded_key_value.shape
 
     bf, f32 = jnp.bfloat16, jnp.float32
@@ -477,12 +508,13 @@
         ((2, keys, HEAD_WIDTH), bf),
         (span_queries.shape, bf),
         ((2, rows, HEAD_WIDTH), bf),
-        (one + dq.shape, bf),
+        (one + halves, bf),
         ((SIDE, 2, keys, HEAD_WIDTH), bf),
         ((SIDE, 2, rows, HEAD_WIDTH), bf),
         ((keys, 2 * HEAD_WIDTH), bf),
-        (two + dq.shape, bf),
-        (decoded, bf), ((2, KEY_HEADS, 2 * steps * requests, HEAD_WIDTH), f32),
+        (two + halves, bf),
+        (decoded, bf), (decode_query.shape, bf),
+        ((2, KEY_HEADS, 2 * steps * requests, HEAD_WIDTH), f32),
         (block_pool_key_value.shape, bf),
         ((SIDE, block, 2 * HEAD_WIDTH), f32),
         (one + part, f32),
@@ -490,16 +522,17 @@
         (one + part, bf), (one + stat, f32),
         (one + part, bf), (one + stat, f32),
         (two + z_part, bf), (two + y_part, bf),
-        (one + z_stat, f32), (one + y_stat, f32),
-        (two + z_part, bf), (one + z_stat, f32),
+        (one + z_stat, f32), (one + z_stat, f32), (one + y_stat, f32),
+        (two + z_part, bf), (one + z_stat, f32), (one + z_stat, f32),
         (two + y_part, bf), (one + y_stat, f32),
         (one + z_part, bf), (one + z_stat, f32),
         (one + z_part, bf), (one + z_stat, f32),
         (one + y_part, bf), (one + y_stat, f32),
         (one + y_part, bf), (one + y_stat, f32),
         (part, f32), (stat, f32),
+        ((block + rows, HEAD_WIDTH), f32),
     ]
-    pairs = [one, (SIDE, 2), one, two, (SIDE, 2), (SIDE, 2), two, one, two, one, (SIDE, 2), (SIDE, 2)]
+    pairs = [one, (SIDE, 2), one, two, (SIDE, 2), (SIDE, 2), two, one, one, two, one, (SIDE, 2), (SIDE, 2)]
     semaphores = [dma((6,))]
     for shape in pairs:
         semaphores += [dma(shape), dma(shape)]
@@ -507,7 +540,7 @@
         fused_kernel,
         out_shape=(
             jax.ShapeDtypeStruct(span_queries.shape, bf),
-            jax.ShapeDtypeStruct(part, bf),
+            jax.ShapeDtypeStruct(decode_query.shape, bf),
         ),
         in_specs=[hbm, hbm, hbm, smem, hbm, smem, smem, smem, hbm, hbm],
         out_specs=(vmem, vmem),
@@ -517,9 +550,7 @@
         ),
         name="span_and_decode",
     )(span_queries, span_key_value, prompt_key_value, span_start, block_pool_key_value, block_dest[:, 0],
-      block_request, block_fill, dq, decoded_key_value)
-    dec = dec.reshape(KEY_HEADS, requests, steps, HEAD_GROUP, HEAD_WIDTH)
-    dec = dec.transpose(2, 1, 0, 3, 4).reshape(steps, requests, QUERY_HEADS * HEAD_WIDTH)
+      block_request, block_fill, decode_query, decoded_key_value)
     return attended, dec
 
 

time: 67.4 us -> 65.7 us (0.975)
  local copies, waits for them, and re-layouts: 4.88 us -> 3.22 us
    reshape x3 -> x0, local copies, waits for them, and re-layouts: 2.39 us -> none  [the longest x2 1.7 us: on_device(): decode_query.reshape(steps, requests, KEY_HEADS, HEAD_GROUP, HEAD_WIDTH)]
    unnamed x1 -> x2, local copies, waits for them, and re-layouts: 1.57 us -> 3.22 us
    transpose x1 -> x0, local copies, waits for them, and re-layouts: 0.93 us -> none  [on_device(): dec.transpose(2, 1, 0, 3, 4)]
where the time goes in v4:
time: 65.7 us; the launch traced here: 65.5 us
  Pallas kernels  61 us (93%)
  local copies, waits for them, and re-layouts  3.22 us (5%)
  between operations  1.29 us (2%)
    pallas_call x1, Pallas kernels, on_device(): pl.pallas_call(fused_kernel, out_shape=(jax.ShapeDtypeStruct(span_queries...  61 us
    unnamed x2, local copies, waits for them, and re-layouts  3.22 us

profile of v4, /device:TPU:0, one launch (start us, length us, event | category | flops | bytes accessed | tf_op | source)
XLA Modules:
  0.0 65.5 jit_solution(14422233400902978786)
XLA Ops:
  1.3 61.0 %span_and_decode.1 = (bf16[64,1024]{1,0:T(8,128)(2,1)}, bf16[4,2,8192]{2,1,0:T(2,128)(2,1)}) custom-call(bf16[64,1024]{1,0:T(8,128)(2,1)} %sq_ref.1, bf16[2,64,128]{2,1,0:T(8,128)(2,1)} %skv_ref.1, bf16[2,1024,128]{2,1,0:T(8,128)(2,1)} %pkv_ref.1, s32[1]{0:T(128)S(6)} %copy.14.start_ref, bf16[16,2,64,1024]{3,2,1,0:T(8,128)(2,1)} %pool_ref.1, s32[16]{0:T(128)} %bitcast.1, ...), custom_call_target="tpu_custom_call" | custom-call | tf_op jit(solution)/shard_map/span_and_decode/pallas_call | solution.py:539
  62.3 1.6 %copy.15 = bf16[64,1024]{1,0:T(8,128)(2,1)} copy(bf16[64,1024]{1,0:T(8,128)(2,1)} %get-tuple-element.4) | data formatting | bytes 262144
  63.8 1.6 %copy.16 = bf16[4,2,8192]{2,1,0:T(2,128)(2,1)} copy(bf16[4,2,8192]{2,1,0:T(2,128)(2,1)} %get-tuple-element.5) | data formatting | bytes 262144

commit v5 on v4

--- a/solution.py
+++ b/solution.py
@@ -19,7 +19,7 @@
 EXP2_SCALE = HEAD_WIDTH ** (-0.5) * 1.4426950408889634
 FAR_LAST = (1, 3, 2)
 SPAN_CHUNK = 256
-Z_ROWS = 384
+Z_ROWS = 256
 
 
 def dot_nt(a, b):
@@ -117,12 +117,25 @@
     load_queries.wait()
     for h in range(KEY_HEADS):
         qb[0, h // 4, pl.ds(h % 4 * rows, rows), :] = stage_q[:, pl.ds(h * HEAD_WIDTH, HEAD_WIDTH)]
+    load_prompt.wait()
+    start = start_ref[0]
+    position = me * keys + lax.broadcasted_iota(jnp.int32, (keys, HEAD_WIDTH), 0)
+    own_keys = stage[0].astype(jnp.float32)
+    kv[0, 0] = jnp.where(position < start, own_keys, own_keys[0:1]).astype(jnp.bfloat16)
+    kv[0, 1] = jnp.where(position < start, stage[1].astype(jnp.float32), 0.0).astype(jnp.bfloat16)
+    load_span.wait()
+    kvs[0] = span[...]
     pl.semaphore_wait(barrier, 6)
 
     q_c, d_c, f_c, kv_c, ks_c = {}, {}, {}, {}, {}
     for o in FAR_LAST:
+        d_c[0, o] = send(dqb.at[0, 0], dqb.at[0, o], d_s.at[0, o], d_r.at[0, o], 0, o)
+    for first in (0, 1):
+        for i, o in enumerate(near):
+            c = (first + i) % 2
+            kv_c[o, c] = send(kv.at[0, c], kv.at[o, c], kv_s.at[o, c], kv_r.at[o, c], 0, o)
+    for o in FAR_LAST:
         q_c[o] = send(qb.at[0], qb.at[o], q_s.at[o], q_r.at[o], o, 0)
-        d_c[0, o] = send(dqb.at[0, 0], dqb.at[0, o], d_s.at[0, o], d_r.at[0, o], 0, o)
 
     def pass_queries(oz):
         for o in near:
@@ -137,18 +150,6 @@
 
     pass_queries(0)
 
-    load_prompt.wait()
-    start = start_ref[0]
-    position = me * keys + lax.broadcasted_iota(jnp.int32, (keys, HEAD_WIDTH), 0)
-    own_keys = stage[0].astype(jnp.float32)
-    kv[0, 0] = jnp.where(position < start, own_keys, own_keys[0:1]).astype(jnp.bfloat16)
-    kv[0, 1] = jnp.where(position < start, stage[1].astype(jnp.float32), 0.0).astype(jnp.bfloat16)
-    for first in (0, 1):
-        for i, o in enumerate(near):
-            c = (first + i) % 2
-            kv_c[o, c] = send(kv.at[0, c], kv.at[o, c], kv_s.at[o, c], kv_r.at[o, c], 0, o)
-    load_span.wait()
-    kvs[0] = span[...]
     for o in FAR_LAST:
         ks_c[o] = send(
             span, kvs.at[o], ks_s.at[o], ks_r.at[o], 0, o
@@ -321,11 +322,13 @@
     load_pool.wait()
     home(0, 0)
     for oz in FAR_LAST:
-        home(0, oz)
+        decode_home(0, oz)
     pass_queries_on(0)
     home(1, 0)
     home(3, 0)
     pass_shards_on()
+    for oz in FAR_LAST:
+        send_partials(0, oz)
     for oz in FAR_LAST:
         pass_queries_on(oz)
         home(1, oz)

time: 65.7 us -> 65.6 us (level)
  no operation moved by 1% of the time
where the time goes in v5:
time: 65.6 us; the launch traced here: 65.4 us
  Pallas kernels  60.9 us (93%)
  local copies, waits for them, and re-layouts  3.22 us (5%)
  between operations  1.29 us (2%)
    pallas_call x1, Pallas kernels, on_device(): pl.pallas_call(fused_kernel, out_shape=(jax.ShapeDtypeStruct(span_queries...  60.9 us
    unnamed x2, local copies, waits for them, and re-layouts  3.22 us

profile of v5, /device:TPU:0, one launch (start us, length us, event | category | flops | bytes accessed | tf_op | source)
XLA Modules:
  0.0 65.4 jit_solution(7233606936839765085)
XLA Ops:
  1.3 60.9 %span_and_decode.1 = (bf16[64,1024]{1,0:T(8,128)(2,1)}, bf16[4,2,8192]{2,1,0:T(2,128)(2,1)}) custom-call(bf16[64,1024]{1,0:T(8,128)(2,1)} %sq_ref.1, bf16[2,64,128]{2,1,0:T(8,128)(2,1)} %skv_ref.1, bf16[2,1024,128]{2,1,0:T(8,128)(2,1)} %pkv_ref.1, s32[1]{0:T(128)S(6)} %copy.14.start_ref, bf16[16,2,64,1024]{3,2,1,0:T(8,128)(2,1)} %pool_ref.1, s32[16]{0:T(128)} %bitcast.1, ...), custom_call_target="tpu_custom_call" | custom-call | tf_op jit(solution)/shard_map/span_and_decode/pallas_call | solution.py:542
  62.2 1.6 %copy.15 = bf16[64,1024]{1,0:T(8,128)(2,1)} copy(bf16[64,1024]{1,0:T(8,128)(2,1)} %get-tuple-element.4) | data formatting | bytes 262144
  63.7 1.6 %copy.16 = bf16[4,2,8192]{2,1,0:T(2,128)(2,1)} copy(bf16[4,2,8192]{2,1,0:T(2,128)(2,1)} %get-tuple-element.5) | data formatting | bytes 262144
